TPU v7x, 32 devices: a whole 2x2x4 slice. The times are simulated.
32 devices in a mesh: parts: 2 (over y), tensor: 4 (over z), dp: 4 (over x, core).
Axes of the slice: x: 2, y: 2, z: 4, core: 2. Of those that a mesh axis runs over, the one named last changes fastest.
Arguments:
- inputs: bfloat16 [4096, 8192], P(('parts', 'dp'), 'tensor'), parts along dimension 0, may hold values from -6 to 6
- out_grad: bfloat16 [4096, 4, 2048], P(('parts', 'dp'), None, 'tensor'), parts along dimension 0, may hold values from -6 to 6
- gate_pre: bfloat16 [4096, 28672], P(('parts', 'dp'), 'tensor'), parts along dimension 0, may hold values from -8 to 8
- down_weight: bfloat16 [28672, 8192], P('tensor', 'dp'), may hold values from -0.03125 to 0.03125
- proj_in: bfloat16 [8192, 64], P('tensor'), may hold values from -0.0625 to 0.0625
- proj_out: bfloat16 [28672, 64], P('tensor'), may hold values from -0.09375 to 0.09375
- queries: bfloat16 [256, 4096], P('tensor', 'dp'), may hold values from -0.1875 to 0.1875
Outputs:
- scores: float32 [256, 4096], P('tensor', ('parts', 'dp')), parts along dimension 1
There are 2 independent parts, one for each index of `parts`. A program takes and returns all parts, laid end to end along the dimension named above; an argument that names none is the same for every part. Nothing has to cross between parts.
All inputs are finite; a program needn't handle non-finite values.
Results may differ from a plain program's by a relative error of at most 0.0041.
Values may be sent and summed in bfloat16 or wider, within the bound.
No kernel may reach another device: no remote copies, remote signals or barrier semaphores. Data moves between devices by JAX's collectives and lax.ppermute only.
A program may use at most 320 MiB of HBM per device.

v0:
```python
import functools

import jax
import jax.numpy as jnp
from jax import lax
from jax.experimental import pallas as pl
from jax.experimental.pallas import tpu as pltpu
from jax.sharding import PartitionSpec as P

TILE = 512
RING = 4
VMEM = 60 * 1024 * 1024
ANY = pl.BlockSpec(memory_space=pl.ANY)


def swap(value, axis, size, mask):
    return lax.ppermute(value, axis, [(i, i ^ mask) for i in range(size)])


def split_kernel(first, grad_ref, *refs):
    me = lax.axis_index("dp")
    out_ref = refs[-1]
    blocks = [grad_ref[:, k, :] for k in range(grad_ref.shape[1])]
    bit = 1
    while bit < len(blocks):
        flip = (me & bit) != 0
        blocks = [jnp.where(flip, blocks[k ^ bit], blocks[k]) for k in range(len(blocks))]
        bit *= 2
    for k in range(out_ref.shape[0]):
        out_ref[k] = blocks[first + k].T


def split_blocks(out_grad, first, after):
    rows, n, width = out_grad.shape
    step = rows // 4
    return pl.pallas_call(
        functools.partial(split_kernel, first),
        grid=(4,),
        in_specs=[pl.BlockSpec((step, n, width), lambda i: (i, 0, 0))] + [ANY] * len(after),
        out_specs=pl.BlockSpec((n // 2, width, step), lambda i: (0, 0, i)),
        out_shape=jax.ShapeDtypeStruct((n // 2, width, rows), out_grad.dtype),
        compiler_params=pltpu.CompilerParams(vmem_limit_bytes=VMEM),
        name="split_blocks",
    )(out_grad, *after)


def gated(hidden, gate_ref, proj_ref):
    gate = gate_ref[...].T.astype(jnp.float32)
    silu = gate * (0.5 + 0.5 * jnp.tanh(0.5 * gate))
    up_grad = (hidden * silu).astype(jnp.bfloat16)
    return jnp.dot(proj_ref[...], up_grad, preferred_element_type=jnp.float32)


def project_kernel(tiles, ahead, pieces, chained, *refs):
    grads = refs[:pieces]
    gate_ref, own_ref, near_ref, proj_ref = refs[pieces : pieces + 4]
    before_ref = refs[pieces + 4] if chained else None
    later_ref = refs[-6] if ahead else None
    out_ref = refs[-7] if ahead else refs[-6]
    rows_ref, even_ref, odd_ref, sum_ref, sems = refs[-5:]
    step = pl.program_id(0)
    pair, width, _ = grads[0].shape

    def fill():
        shard = lax.axis_index("tensor")
        copies = []
        for k, grad_ref in enumerate(grads):
            place = slice(None)
            if pieces > 1:
                place = pl.ds(pl.multiple_of(lax.rem(shard + pieces - k, pieces) * width, width), width)
            for p in range(pair):
                copies.append(
                    pltpu.make_async_copy(grad_ref.at[p], rows_ref.at[p, place], sems.at[k, p])
                )
        for copy in copies:
            copy.start()
        sum_ref[...] = jnp.zeros_like(sum_ref)
        for copy in copies:
            copy.wait()

    def multiply(hidden_ref):
        hidden_ref[...] = jnp.dot(
            own_ref[...], rows_ref[0], preferred_element_type=jnp.float32
        ) + jnp.dot(near_ref[...], rows_ref[1], preferred_element_type=jnp.float32)

    def reduce(hidden_ref):
        sum_ref[...] += gated(hidden_ref[...], gate_ref, proj_ref)

    @pl.when(step == 0)
    def _():
        fill()
        multiply(even_ref)

    @pl.when((step > 0) & (step < tiles) & (lax.rem(step, 2) == 1))
    def _():
        reduce(even_ref)
        multiply(odd_ref)

    @pl.when((step > 0) & (step < tiles) & (lax.rem(step, 2) == 0))
    def _():
        reduce(odd_ref)
        multiply(even_ref)

    @pl.when(step == tiles)
    def _():
        reduce(even_ref if tiles % 2 else odd_ref)
        total = sum_ref[...]
        out_ref[...] = total + before_ref[...] if chained else total
        if ahead:
            multiply(later_ref)

    if ahead > 1:

        @pl.when(step > tiles)
        def _():
            multiply(later_ref)


def project(grads, gate, weights, proj, offset, span, extra, gate_column, before, after):
    pieces = len(grads)
    pair, _, rows = grads[0].shape
    depth = weights[0].shape[1]
    k = proj.shape[0]
    tile = TILE if span % TILE == 0 else span
    tiles = span // tile
    ahead = extra // tile
    first, gate_first = offset // tile, gate_column // tile
    now = lambda i: first + jnp.minimum(i, tiles + ahead - 1)
    last = lambda i: jnp.clip(i - 1, 0, tiles - 1)
    chained = before is not None
    total = pl.BlockSpec((k, rows), lambda i: (0, 0))
    later = pl.BlockSpec((tile, rows), lambda i: (jnp.maximum(i - tiles, 0), 0))
    return pl.pallas_call(
        functools.partial(project_kernel, tiles, ahead, pieces, chained),
        grid=(tiles + max(ahead, 1),),
        in_specs=[ANY] * pieces
        + [
            pl.BlockSpec((rows, tile), lambda i: (0, gate_first + last(i))),
            pl.BlockSpec((tile, depth), lambda i: (now(i), 0)),
            pl.BlockSpec((tile, depth), lambda i: (now(i), 0)),
            pl.BlockSpec((k, tile), lambda i: (0, first + last(i))),
        ]
        + [total] * chained
        + [ANY] * len(after),
        out_specs=[total] + [later] * bool(ahead),
        out_shape=[jax.ShapeDtypeStruct((k, rows), jnp.float32)]
        + [jax.ShapeDtypeStruct((extra, rows), jnp.float32)] * bool(ahead),
        scratch_shapes=[
            pltpu.VMEM((pair, depth, rows), grads[0].dtype),
            pltpu.VMEM((tile, rows), jnp.float32),
            pltpu.VMEM((tile, rows), jnp.float32),
            pltpu.VMEM((k, rows), jnp.float32),
            pltpu.SemaphoreType.DMA((pieces, pair)),
        ],
        compiler_params=pltpu.CompilerParams(vmem_limit_bytes=VMEM),
        cost_estimate=pl.CostEstimate(
            flops=2 * rows * (span + extra) * (pair * depth + 4 * k),
            bytes_accessed=2 * (span + extra) * (pair * depth + rows),
            transcendentals=rows * span,
        ),
        name="project",
    )(*grads, gate, *weights, proj, *([before] if chained else []), *after)


def finish_kernel(hidden_ref, gate_ref, proj_ref, before_ref, *refs):
    out_ref = refs[-1]

    @pl.when(pl.program_id(0) == 0)
    def _():
        out_ref[...] = before_ref[...]

    out_ref[...] += gated(hidden_ref[...], gate_ref, proj_ref)


def finish(hidden, gate, proj, offset, before, after):
    span, rows = hidden.shape
    k = proj.shape[0]
    first = offset // TILE
    total = pl.BlockSpec((k, rows), lambda i: (0, 0))
    return pl.pallas_call(
        finish_kernel,
        grid=(span // TILE,),
        in_specs=[
            pl.BlockSpec((TILE, rows), lambda i: (i, 0)),
            pl.BlockSpec((rows, TILE), lambda i: (0, i)),
            pl.BlockSpec((k, TILE), lambda i: (0, first + i)),
            total,
        ]
        + [ANY] * len(after),
        out_specs=total,
        out_shape=jax.ShapeDtypeStruct((k, rows), jnp.float32),
        compiler_params=pltpu.CompilerParams(vmem_limit_bytes=VMEM),
        name="finish",
    )(hidden, gate, proj, before, *after)


def score_kernel(input_ref, grad_ref, other_ref, query_ref, out_ref):
    grad = grad_ref[...] + other_ref[...]
    high = grad.astype(jnp.bfloat16)
    low = (grad - high.astype(jnp.float32)).astype(jnp.bfloat16)
    both = jnp.concatenate([high, low], axis=0)
    total = jnp.zeros_like(out_ref)
    for i in range(query_ref.shape[0]):
        part = jnp.dot(query_ref[i], both, preferred_element_type=jnp.float32)
        total += input_ref[i : i + 1, :] * part
    out_ref[...] = total


def pair_queries(queries, k):
    pairs = queries.reshape(queries.shape[0], k, k).transpose(1, 0, 2)
    return jnp.concatenate([pairs, pairs], axis=2)


def score(input_proj, grad, other, pairs):
    return pl.pallas_call(
        score_kernel,
        out_shape=jax.ShapeDtypeStruct((pairs.shape[1], grad.shape[1]), jnp.float32),
        compiler_params=pltpu.CompilerParams(vmem_limit_bytes=VMEM),
        name="score",
    )(input_proj, grad, other, pairs)


def chunks_of(hidden):
    units = hidden // TILE
    last = 3 * TILE if hidden % TILE == 0 and units >= 8 else 0
    return hidden - last, last


def on_device(n_dp, n_tensor, inputs, out_grad, gate_pre, down_weight, proj_in, proj_out, queries):
    rows = out_grad.shape[0]
    hidden = gate_pre.shape[1]
    me = lax.axis_index("dp")
    far, near = n_dp // 2, 1

    def gather(block, holds):
        if n_tensor > RING:
            grad = lax.all_gather(block, "tensor", axis=0, tiled=False)
            return [jnp.transpose(grad, (1, 0, 2, 3)).reshape(2, -1, rows)]
        pieces = [block]
        for k in range(n_tensor - 1):
            piece = pieces[-1]
            if k in holds:
                piece, _ = lax.optimization_barrier((piece, holds[k]))
                pieces[-1] = piece
            pieces.append(
                lax.ppermute(piece, "tensor", [(i, (i + 1) % n_tensor) for i in range(n_tensor)])
            )
        return pieces

    main, extra = chunks_of(hidden)
    weights = (down_weight, swap(down_weight, "dp", n_dp, near))

    far_query = swap(queries, "dp", n_dp, far)
    near_query = swap(queries, "dp", n_dp, near)
    diag_query = swap(far_query, "dp", n_dp, near)

    far_blocks = split_blocks(out_grad, n_dp // 2, ())
    own_blocks = split_blocks(out_grad, 0, (far_blocks,))
    far_blocks, _ = lax.optimization_barrier((far_blocks, far_query))
    far_start = swap(far_blocks, "dp", n_dp, far)
    gates, far_start = lax.optimization_barrier(
        ((gate_pre[:, :main], gate_pre[:, main:]), far_start)
    )
    far_gate, last_gate = (swap(part, "dp", n_dp, far) if part.size else None for part in gates)
    grads_own = gather(own_blocks, {})

    input_proj = lax.dot_general(
        proj_in, inputs, (((0,), (1,)), ((), ())), preferred_element_type=jnp.float32
    )
    width = queries.shape[1]
    all_queries = jnp.zeros((queries.shape[0], n_dp * width), queries.dtype)
    for mask, block in enumerate((queries, near_query, far_query, diag_query)):
        all_queries = lax.dynamic_update_slice(all_queries, block, (0, (me ^ mask) * width))
    pairs = pair_queries(all_queries, proj_in.shape[1])

    middle = hidden // 2 if hidden % (2 * TILE) == 0 else hidden
    proj_out = proj_out.T
    own_sum = None
    after = ()
    for s in range(0, hidden, middle):
        (own_sum,) = project(
            grads_own, gate_pre, weights, proj_out, s, middle, 0, s, own_sum, after
        )
        if s == 0:
            grads_far = gather(far_start, {2: own_sum})
        after = (own_sum,)
    input_proj, own_sum = lax.optimization_barrier((input_proj, own_sum))
    mask = 1
    while mask < n_tensor:
        input_proj = input_proj + swap(input_proj, "tensor", n_tensor, mask)
        mask *= 2
    far_sum, *later = project(
        grads_far, far_gate, weights, proj_out, 0, main, extra, 0, None, (own_sum,)
    )
    if extra:
        far_sum = finish(later[0], last_gate, proj_out, main, far_sum, (pairs, input_proj))

    value = own_sum + swap(far_sum, "dp", n_dp, far)
    mask = 1
    while mask < n_tensor:
        other = swap(value, "tensor", n_tensor, mask)
        mask *= 2
        if mask < n_tensor:
            value = value + other
    return score(input_proj, value, other, pairs)


def solution(mesh):
    return jax.shard_map(
        functools.partial(on_device, mesh.shape["dp"], mesh.shape["tensor"]),
        mesh=mesh,
        in_specs=(
            P(("parts", "dp"), "tensor"),
            P(("parts", "dp"), None, "tensor"),
            P(("parts", "dp"), "tensor"),
            P("tensor", "dp"),
            P("tensor", None),
            P("tensor", None),
            P("tensor", "dp"),
        ),
        out_specs=P("tensor", ("parts", "dp")),
        check_vma=False,
    )
```

profile of v0, /device:TPU:0, one launch (start us, length us, event | category | flops | bytes accessed | tf_op | source)
XLA Modules:
  0.0 250.3 jit_solution(7558880828257151752)
XLA Ops:
  0.0 0.0 copy-start
  0.0 0.5 collective-permute-start.3
  0.5 2.6 %collective-permute-start.6 = (bf16[64,1024]{1,0:T(8,128)(2,1)}, bf16[64,1024]{1,0:T(8,128)(2,1)S(1)}, u32[]{:S(2)}, u32[]{:S(2)}) collective-permute-start(bf16[64,1024]{1,0:T(8,128)(2,1)} %param.13), channel_id=1, source_target_pairs={{0,2},{1,3},{2,0},{3,1},{4,6},{5,7},{6,4},{7,5},{8,10},{9,11},{10,... | collective-permute-start | bytes 393224 | tf_op jit(solution)/shard_map/ppermute | solution.py:17
  3.0 5.4 %split_blocks.2.refs_0_ = bf16[2,512,512]{2,1,0:T(8,128)(2,1)} custom-call(bf16[512,4,512]{2,1,0:T(4,128)(2,1)} %grad_ref.3), custom_call_target="tpu_custom_call" | custom-call | tf_op jit(solution)/shard_map/split_blocks/pallas_call | solution.py:36
  8.4 0.0 collective-permute-done.6
  8.4 0.7 collective-permute-start.7
  9.1 5.4 %split_blocks.3.refs_0_ = bf16[2,512,512]{2,1,0:T(8,128)(2,1)} custom-call(bf16[512,4,512]{2,1,0:T(4,128)(2,1)} %grad_ref.3, bf16[2,512,512]{2,1,0:T(8,128)(2,1)} %split_blocks.2.refs_0_), custom_call_target="tpu_custom_call" | custom-call | tf_op jit(solution)/shard_map/split_blocks/pallas_call | solution.py:36
  14.4 1.6 collective-permute-start
  16.0 2.7 %slice.7 = bf16[512,1536]{1,0:T(8,128)(2,1)} slice(bf16[512,7168]{1,0:T(8,128)(2,1)} %refs_4_.3), slice={[0:512], [5632:7168]} | slice | bytes 3145728 | tf_op jit(solution)/shard_map/slice | solution.py:262
  18.7 0.0 copy-start.8
  18.7 5.5 %slice.6 = bf16[512,5632]{1,0:T(8,128)(2,1)} slice(bf16[512,7168]{1,0:T(8,128)(2,1)} %refs_4_.3), slice={[0:512], [0:5632]} | slice | bytes 11534336 | tf_op jit(solution)/shard_map/slice | solution.py:262
  24.2 9.7 %collective-permute-done.7.refs_0_ = bf16[2,512,512]{2,1,0:T(8,128)(2,1)} collective-permute-done((bf16[2,512,512]{2,1,0:T(8,128)(2,1)}, bf16[2,512,512]{2,1,0:T(8,128)(2,1)}, u32[]{:S(2)}, u32[]{:S(2)}) %collective-permute-start.7) | collective-permute-done | bytes 1048608 | tf_op jit(solution)/shard_map/ppermute | solution.py:17
  33.9 0.3 collective-permute-start.11
  34.2 7.1 %collective-permute-done.refs_1_ = bf16[2,512,512]{2,1,0:T(8,128)(2,1)S(1)} collective-permute-done((bf16[2,512,512]{2,1,0:T(8,128)(2,1)}, bf16[2,512,512]{2,1,0:T(8,128)(2,1)S(1)}, u32[]{:S(2)}, u32[]{:S(2)}) %collective-permute-start) | collective-permute-done | bytes 1048608 | tf_op jit(solution)/shard_map/ppermute | solution.py:246
  41.3 0.0 collective-permute-start.1
  41.3 1.3 collective-permute-start.8
  42.6 26.7 %collective-permute-done.1.refs_2_ = bf16[2,512,512]{2,1,0:T(8,128)(2,1)} collective-permute-done((bf16[2,512,512]{2,1,0:T(8,128)(2,1)S(1)}, bf16[2,512,512]{2,1,0:T(8,128)(2,1)}, u32[]{:S(2)}, u32[]{:S(2)}) %collective-permute-start.1) | collective-permute-done | bytes 1048608 | tf_op jit(solution)/shard_map/ppermute | solution.py:246
  69.3 0.0 collective-permute-start.2
  69.3 0.0 copy-done.8
  69.3 0.0 collective-permute-start.13
  69.3 0.0 copy-done
  69.3 0.0 copy-done.6
  69.3 0.8 fusion
  70.2 0.6 collective-permute-done.13
  70.8 0.1 collective-permute-start.14
  70.9 0.9 constant_dynamic-update-slice_fusion.2
  71.8 19.9 %collective-permute-done.8.refs_1_ = bf16[2,512,512]{2,1,0:T(8,128)(2,1)} collective-permute-done((bf16[2,512,512]{2,1,0:T(8,128)(2,1)}, bf16[2,512,512]{2,1,0:T(8,128)(2,1)}, u32[]{:S(2)}, u32[]{:S(2)}) %collective-permute-start.8) | collective-permute-done | bytes 1048608 | tf_op jit(solution)/shard_map/ppermute | solution.py:246
  91.8 0.0 collective-permute-start.9
  91.8 22.5 %collective-permute-done.2.refs_3_ = bf16[2,512,512]{2,1,0:T(8,128)(2,1)} collective-permute-done((bf16[2,512,512]{2,1,0:T(8,128)(2,1)}, bf16[2,512,512]{2,1,0:T(8,128)(2,1)}, u32[]{:S(2)}, u32[]{:S(2)}) %collective-permute-start.2) | collective-permute-done | bytes 1048608 | tf_op jit(solution)/shard_map/ppermute | solution.py:246
  114.2 0.0 collective-permute-done.3.refs_6_
  114.2 0.0 copy-done.2
  114.2 24.9 %project.3.refs_8_.refs_9_ = f32[64,512]{1,0:T(8,128)} custom-call(bf16[2,512,512]{2,1,0:T(8,128)(2,1)} %split_blocks.3.refs_0_, bf16[2,512,512]{2,1,0:T(8,128)(2,1)} %copy-done.2, bf16[2,512,512]{2,1,0:T(8,128)(2,1)} %collective-permute-done.1.refs_2_, bf16[2,512,512]{2,1,0:T(8,128)(2,1)} %collective-permute-done.2.refs_3_, bf16[512,7168]{1,0:T(8,128)(2,1)} %refs_4_.3, ...), custom_call_target="tpu_custom_call" | custom-call | flops 15971909632 | bytes 33030144 | tf_op jit(solution)/shard_map/project/pallas_call | solution.py:133
  139.2 0.0 collective-permute-done.9.refs_2_
  139.2 0.2 collective-permute-start.10
  139.4 25.3 %project.4.refs_8_ = f32[64,512]{1,0:T(8,128)} custom-call(bf16[2,512,512]{2,1,0:T(8,128)(2,1)} %split_blocks.3.refs_0_, bf16[2,512,512]{2,1,0:T(8,128)(2,1)} %copy-done.2, bf16[2,512,512]{2,1,0:T(8,128)(2,1)} %collective-permute-done.1.refs_2_, bf16[2,512,512]{2,1,0:T(8,128)(2,1)} %collective-permute-done.2.refs_3_, bf16[512,7168]{1,0:T(8,128)(2,1)} %refs_4_.3, ...), custom_call_target="tpu_custom_call" | custom-call | flops 15971909632 | bytes 33030144 | tf_op jit(solution)/shard_map/project/pallas_call | solution.py:133
  164.7 0.1 collective-permute-start.4
  164.8 0.0 collective-permute-done.14
  164.9 1.1 reshape.3
  166.0 0.7 copy.10
  166.7 3.9 %collective-permute-done.4 = f32[64,512]{1,0:T(8,128)S(1)} collective-permute-done((f32[64,512]{1,0:T(8,128)S(1)}, f32[64,512]{1,0:T(8,128)S(1)}, u32[]{:S(2)}, u32[]{:S(2)}) %collective-permute-start.4) | collective-permute-done | bytes 131104 | tf_op jit(solution)/shard_map/ppermute | solution.py:17
  170.6 2.3 collective-permute-start.5
  172.9 1.6 pad_maximum_fusion.refs_0_.query_ref
  174.5 1.7 collective-permute-start.12
  176.2 1.8 collective-permute-done.5
  177.9 0.7 add.25.refs_1_.input_ref
  178.6 0.0 collective-permute-done.11.refs_4_
  178.6 0.0 collective-permute-done.10.refs_3_
  178.6 43.8 %project.5 = (f32[64,512]{1,0:T(8,128)}, f32[1536,512]{1,0:T(8,128)}) custom-call(bf16[2,512,512]{2,1,0:T(8,128)(2,1)} %collective-permute-done.7.refs_0_, bf16[2,512,512]{2,1,0:T(8,128)(2,1)} %collective-permute-done.8.refs_1_, bf16[2,512,512]{2,1,0:T(8,128)(2,1)} %collective-permute-done.9.refs_2_, bf16[2,512,512]{2,1,0:T(8,128)(2,1)} %collective-permute-done.10.refs_3_, ...), custom_call_target="tpu_custom_call" | custom-call | flops 31943819264 | bytes 66060288 | tf_op jit(solution)/shard_map/project/pallas_call | solution.py:133
  222.4 0.0 collective-permute-done.12.gate_ref
  222.5 0.0 copy-start.3
  222.5 1.2 copy-done.3
  223.6 5.0 %finish.1 = f32[64,512]{1,0:T(8,128)} custom-call(f32[1536,512]{1,0:T(8,128)} %get-tuple-element.20.hidden_ref, bf16[512,1536]{1,0:T(8,128)(2,1)} %copy-done.3, bf16[64,7168]{1,0:T(8,128)(2,1)} %bitcast.9, f32[64,512]{1,0:T(8,128)} %get-tuple-element.22.before_ref, bf16[64,64,128]{2,1,0:T(8,128)(2,1)} %pad_maximum_fusion.refs_0_.query_ref, ...), custom_call_target="tpu_custom_call" | custom-call | tf_op jit(solution)/shard_map/finish/pallas_call | solution.py:180
  228.7 2.1 collective-permute-start.15
  230.7 3.2 %collective-permute-done.15 = f32[64,512]{1,0:T(8,128)S(1)} collective-permute-done((f32[64,512]{1,0:T(8,128)}, f32[64,512]{1,0:T(8,128)S(1)}, u32[]{:S(2)}, u32[]{:S(2)}) %collective-permute-start.15) | collective-permute-done | bytes 131104 | tf_op jit(solution)/shard_map/ppermute | solution.py:17
  233.9 0.0 copy-done.4
  233.9 0.7 collective-permute-start.16
  234.6 4.3 %collective-permute-done.16 = f32[64,512]{1,0:T(8,128)S(1)} collective-permute-done((f32[64,512]{1,0:T(8,128)S(1)}, f32[64,512]{1,0:T(8,128)S(1)}, u32[]{:S(2)}, u32[]{:S(2)}) %collective-permute-start.16) | collective-permute-done | bytes 131104 | tf_op jit(solution)/shard_map/ppermute | solution.py:17
  239.0 0.0 copy-start.5
  239.0 1.7 collective-permute-start.17
  240.7 5.6 %collective-permute-done.17.other_ref = f32[64,512]{1,0:T(8,128)S(1)} collective-permute-done((f32[64,512]{1,0:T(8,128)S(1)}, f32[64,512]{1,0:T(8,128)S(1)}, u32[]{:S(2)}, u32[]{:S(2)}) %collective-permute-start.17) | collective-permute-done | bytes 131104 | tf_op jit(solution)/shard_map/ppermute | solution.py:17
  246.3 0.0 copy-done.5
  246.3 0.6 copy-done.7
  247.0 3.3 %score.1 = f32[64,512]{1,0:T(8,128)} custom-call(f32[64,512]{1,0:T(8,128)} %add.25.refs_1_.input_ref, f32[64,512]{1,0:T(8,128)} %copy-done.5, f32[64,512]{1,0:T(8,128)} %copy-done.7, bf16[64,64,128]{2,1,0:T(8,128)(2,1)} %pad_maximum_fusion.refs_0_.query_ref), custom_call_target="tpu_custom_call" | custom-call | tf_op jit(solution)/shard_map/score/pallas_call | solution.py:215
  250.3 0.0 copy-done.1
  (12 shorter events, 0.2 us)
Async XLA Ops:
  0.0 69.3 %copy-start = (bf16[512,2048]{1,0:T(8,128)(2,1)S(1)}, bf16[512,2048]{1,0:T(8,128)(2,1)}, u32[]{:S(2)}) copy-start(bf16[512,2048]{1,0:T(8,128)(2,1)} %param.7) | copy-start | bytes 6291460
  0.0 114.2 %collective-permute-start.3 = (bf16[7168,2048]{1,0:T(8,128)(2,1)}, bf16[7168,2048]{1,0:T(8,128)(2,1)}, u32[]{:S(2)}, u32[]{:S(2)}) collective-permute-start(bf16[7168,2048]{1,0:T(8,128)(2,1)} %refs_5_.5), channel_id=1, source_target_pairs={{0,1},{1,0},{2,3},{3,2},{4,5},{5,4},{6,7},{7,6},{8,9},{9,8},{10,11... | collective-permute-start | bytes 88080392 | tf_op jit(solution)/shard_map/ppermute | solution.py:17
  0.5 7.9 %collective-permute-start.6 = (bf16[64,1024]{1,0:T(8,128)(2,1)}, bf16[64,1024]{1,0:T(8,128)(2,1)S(1)}, u32[]{:S(2)}, u32[]{:S(2)}) collective-permute-start(bf16[64,1024]{1,0:T(8,128)(2,1)} %param.13), channel_id=1, source_target_pairs={{0,2},{1,3},{2,0},{3,1},{4,6},{5,7},{6,4},{7,5},{8,10},{9,11},{10,... | collective-permute-start | bytes 393224 | tf_op jit(solution)/shard_map/ppermute | solution.py:17
  8.4 25.5 %collective-permute-start.7 = (bf16[2,512,512]{2,1,0:T(8,128)(2,1)}, bf16[2,512,512]{2,1,0:T(8,128)(2,1)}, u32[]{:S(2)}, u32[]{:S(2)}) collective-permute-start(bf16[2,512,512]{2,1,0:T(8,128)(2,1)} %split_blocks.2.refs_0_), channel_id=1, source_target_pairs={{0,2},{1,3},{2,0},{3,1},{4,6},{5,7},{6,4},{7,5},{8,10},{9,11},{10,... | collective-permute-start | bytes 3145736 | tf_op jit(solution)/shard_map/ppermute | solution.py:17
  14.4 26.9 %collective-permute-start = (bf16[2,512,512]{2,1,0:T(8,128)(2,1)}, bf16[2,512,512]{2,1,0:T(8,128)(2,1)S(1)}, u32[]{:S(2)}, u32[]{:S(2)}) collective-permute-start(bf16[2,512,512]{2,1,0:T(8,128)(2,1)} %split_blocks.3.refs_0_), channel_id=1, source_target_pairs={{0,4},{4,8},{8,12},{12,0},{1,5},{5,9},{9,13},{13,1},{2,6},{6,10},{... | collective-permute-start | bytes 3145736 | tf_op jit(solution)/shard_map/ppermute | solution.py:246
  18.7 50.6 %copy-start.8 = (bf16[64,1024]{1,0:T(8,128)(2,1)S(1)}, bf16[64,1024]{1,0:T(8,128)(2,1)}, u32[]{:S(2)}) copy-start(bf16[64,1024]{1,0:T(8,128)(2,1)} %param.13) | copy-start | bytes 393220
  18.7 50.6 %copy-start.6 = (bf16[2048,64]{0,1:T(8,128)(2,1)S(1)}, bf16[2048,64]{0,1:T(8,128)(2,1)}, u32[]{:S(2)}) copy-start(bf16[2048,64]{0,1:T(8,128)(2,1)} %param.11) | copy-start | bytes 786436
  33.9 144.7 %collective-permute-start.11 = (bf16[512,5632]{1,0:T(8,128)(2,1)}, bf16[512,5632]{1,0:T(8,128)(2,1)}, u32[]{:S(2)}, u32[]{:S(2)}) collective-permute-start(bf16[512,5632]{1,0:T(8,128)(2,1)} %slice.6), channel_id=1, source_target_pairs={{0,2},{1,3},{2,0},{3,1},{4,6},{5,7},{6,4},{7,5},{8,10},{9,11},{10,... | collective-permute-start | bytes 17301512 | tf_op jit(solution)/shard_map/ppermute | solution.py:17
  41.3 72.9 %copy-start.2 = (bf16[2,512,512]{2,1,0:T(8,128)(2,1)}, bf16[2,512,512]{2,1,0:T(8,128)(2,1)S(1)}, u32[]{:S(2)}) copy-start(bf16[2,512,512]{2,1,0:T(8,128)(2,1)S(1)} %collective-permute-done.refs_1_) | copy-start | bytes 3145732
  41.3 28.0 %collective-permute-start.1 = (bf16[2,512,512]{2,1,0:T(8,128)(2,1)S(1)}, bf16[2,512,512]{2,1,0:T(8,128)(2,1)}, u32[]{:S(2)}, u32[]{:S(2)}) collective-permute-start(bf16[2,512,512]{2,1,0:T(8,128)(2,1)S(1)} %collective-permute-done.refs_1_), channel_id=1, source_target_pairs={{0,4},{4,8},{8,12},{12,0},{1,5},{5,9},{9,13},{13,1},{2,6},{6,10},{... | collective-permute-start | bytes 3145736 | tf_op jit(solution)/shard_map/ppermute | solution.py:246
  41.3 50.5 %collective-permute-start.8 = (bf16[2,512,512]{2,1,0:T(8,128)(2,1)}, bf16[2,512,512]{2,1,0:T(8,128)(2,1)}, u32[]{:S(2)}, u32[]{:S(2)}) collective-permute-start(bf16[2,512,512]{2,1,0:T(8,128)(2,1)} %collective-permute-done.7.refs_0_), channel_id=1, source_target_pairs={{0,4},{4,8},{8,12},{12,0},{1,5},{5,9},{9,13},{13,1},{2,6},{6,10},{... | collective-permute-start | bytes 3145736 | tf_op jit(solution)/shard_map/ppermute | solution.py:246
  69.3 44.9 %collective-permute-start.2 = (bf16[2,512,512]{2,1,0:T(8,128)(2,1)}, bf16[2,512,512]{2,1,0:T(8,128)(2,1)}, u32[]{:S(2)}, u32[]{:S(2)}) collective-permute-start(bf16[2,512,512]{2,1,0:T(8,128)(2,1)} %collective-permute-done.1.refs_2_), channel_id=1, source_target_pairs={{0,4},{4,8},{8,12},{12,0},{1,5},{5,9},{9,13},{13,1},{2,6},{6,10},{... | collective-permute-start | bytes 3145736 | tf_op jit(solution)/shard_map/ppermute | solution.py:246
  69.3 1.5 collective-permute-start.13
  70.8 94.0 %collective-permute-start.14 = (bf16[64,1024]{1,0:T(8,128)(2,1)S(1)}, bf16[64,1024]{1,0:T(8,128)(2,1)S(1)}, u32[]{:S(2)}, u32[]{:S(2)}) collective-permute-start(bf16[64,1024]{1,0:T(8,128)(2,1)S(1)} %collective-permute-done.6), channel_id=1, source_target_pairs={{0,1},{1,0},{2,3},{3,2},{4,5},{5,4},{6,7},{7,6},{8,9},{9,8},{10,11... | collective-permute-start | bytes 393224 | tf_op jit(solution)/shard_map/ppermute | solution.py:17
  91.8 47.4 %collective-permute-start.9 = (bf16[2,512,512]{2,1,0:T(8,128)(2,1)}, bf16[2,512,512]{2,1,0:T(8,128)(2,1)}, u32[]{:S(2)}, u32[]{:S(2)}) collective-permute-start(bf16[2,512,512]{2,1,0:T(8,128)(2,1)} %collective-permute-done.8.refs_1_), channel_id=1, source_target_pairs={{0,4},{4,8},{8,12},{12,0},{1,5},{5,9},{9,13},{13,1},{2,6},{6,10},{... | collective-permute-start | bytes 3145736 | tf_op jit(solution)/shard_map/ppermute | solution.py:246
  139.2 39.4 %collective-permute-start.10 = (bf16[2,512,512]{2,1,0:T(8,128)(2,1)}, bf16[2,512,512]{2,1,0:T(8,128)(2,1)}, u32[]{:S(2)}, u32[]{:S(2)}) collective-permute-start(bf16[2,512,512]{2,1,0:T(8,128)(2,1)} %collective-permute-done.9.refs_2_), channel_id=1, source_target_pairs={{0,4},{4,8},{8,12},{12,0},{1,5},{5,9},{9,13},{13,1},{2,6},{6,10},{... | collective-permute-start | bytes 3145736 | tf_op jit(solution)/shard_map/ppermute | solution.py:246
  164.7 5.9 %collective-permute-start.4 = (f32[64,512]{1,0:T(8,128)S(1)}, f32[64,512]{1,0:T(8,128)S(1)}, u32[]{:S(2)}, u32[]{:S(2)}) collective-permute-start(f32[64,512]{1,0:T(8,128)S(1)} %fusion), channel_id=1, source_target_pairs={{0,4},{4,0},{8,12},{12,8},{1,5},{5,1},{9,13},{13,9},{2,6},{6,2},{1... | collective-permute-start | bytes 393224 | tf_op jit(solution)/shard_map/ppermute | solution.py:17
  170.6 7.3 %collective-permute-start.5 = (f32[64,512]{1,0:T(8,128)S(1)}, f32[64,512]{1,0:T(8,128)S(1)}, u32[]{:S(2)}, u32[]{:S(2)}) collective-permute-start(f32[64,512]{1,0:T(8,128)S(1)} %add.24), channel_id=1, source_target_pairs={{0,8},{4,12},{8,0},{12,4},{1,9},{5,13},{9,1},{13,5},{2,10},{6,14},... | collective-permute-start | bytes 393224 | tf_op jit(solution)/shard_map/ppermute | solution.py:17
  174.5 48.0 %collective-permute-start.12 = (bf16[512,1536]{1,0:T(8,128)(2,1)}, bf16[512,1536]{1,0:T(8,128)(2,1)S(1)}, u32[]{:S(2)}, u32[]{:S(2)}) collective-permute-start(bf16[512,1536]{1,0:T(8,128)(2,1)} %slice.7), channel_id=1, source_target_pairs={{0,2},{1,3},{2,0},{3,1},{4,6},{5,7},{6,4},{7,5},{8,10},{9,11},{10,... | collective-permute-start | bytes 4718600 | tf_op jit(solution)/shard_map/ppermute | solution.py:17
  222.5 1.2 copy-start.3
  223.6 10.3 %copy-start.4 = (f32[64,512]{1,0:T(8,128)S(1)}, f32[64,512]{1,0:T(8,128)}, u32[]{:S(2)}) copy-start(f32[64,512]{1,0:T(8,128)} %project.4.refs_8_) | copy-start | bytes 393220
  223.6 26.7 %copy-start.1 = (bf16[512,2048]{1,0:T(8,128)(2,1)S(1)}, bf16[512,2048]{1,0:T(8,128)(2,1)}, u32[]{:S(2)}) copy-start(bf16[512,2048]{1,0:T(8,128)(2,1)} %param.7) | copy-start | bytes 6291460
  228.7 5.2 %collective-permute-start.15 = (f32[64,512]{1,0:T(8,128)}, f32[64,512]{1,0:T(8,128)S(1)}, u32[]{:S(2)}, u32[]{:S(2)}) collective-permute-start(f32[64,512]{1,0:T(8,128)} %finish.1), channel_id=1, source_target_pairs={{0,2},{1,3},{2,0},{3,1},{4,6},{5,7},{6,4},{7,5},{8,10},{9,11},{10,... | collective-permute-start | bytes 393224 | tf_op jit(solution)/shard_map/ppermute | solution.py:17
  233.9 5.0 %collective-permute-start.16 = (f32[64,512]{1,0:T(8,128)S(1)}, f32[64,512]{1,0:T(8,128)S(1)}, u32[]{:S(2)}, u32[]{:S(2)}) collective-permute-start(f32[64,512]{1,0:T(8,128)S(1)} %add.30), channel_id=1, source_target_pairs={{0,4},{4,0},{8,12},{12,8},{1,5},{5,1},{9,13},{13,9},{2,6},{6,2},{1... | collective-permute-start | bytes 393224 | tf_op jit(solution)/shard_map/ppermute | solution.py:17
  239.0 7.3 %copy-start.5 = (f32[64,512]{1,0:T(8,128)}, f32[64,512]{1,0:T(8,128)S(1)}, u32[]{:S(2)}) copy-start(f32[64,512]{1,0:T(8,128)S(1)} %add.31.grad_ref) | copy-start | bytes 393220
  239.0 7.3 %collective-permute-start.17 = (f32[64,512]{1,0:T(8,128)S(1)}, f32[64,512]{1,0:T(8,128)S(1)}, u32[]{:S(2)}, u32[]{:S(2)}) collective-permute-start(f32[64,512]{1,0:T(8,128)S(1)} %add.31.grad_ref), channel_id=1, source_target_pairs={{0,8},{4,12},{8,0},{12,4},{1,9},{5,13},{9,1},{13,5},{2,10},{6,14},... | collective-permute-start | bytes 393224 | tf_op jit(solution)/shard_map/ppermute | solution.py:17
  246.3 0.6 copy-start.7
where the time goes:
time: 251 us; the launch traced here: 250 us
  Pallas kernels  113 us (45%)
  waiting for transfers between devices  105 us (42%)
  starting transfers between devices  15.8 us (6%)
  local copies, waits for them, and re-layouts  12.8 us (5%)
    pallas_call x3, Pallas kernels, project(): pl.pallas_call(functools.partial(project_kernel, tiles, ahead, pieces, ch...  94 us
    ppermute x6, waiting for transfers between devices, gather(): lax.ppermute(piece, 'tensor', [(i, (i + 1) % n_tensor) for i in range(n_t...  76.2 us
    ppermute x12, waiting for transfers between devices, swap(): return lax.ppermute(value, axis, [(i, i ^ mask) for i in range(size)])  29.1 us
    ppermute x12, starting transfers between devices, swap(): return lax.ppermute(value, axis, [(i, i ^ mask) for i in range(size)])  12.7 us
    pallas_call x2, Pallas kernels, split_blocks(): pl.pallas_call(functools.partial(split_kernel, first), grid=(4,), in_spec...  10.7 us
    slice x1, local copies, waits for them, and re-layouts, on_device(): gate_pre[:, :main]  5.49 us
    pallas_call x1, Pallas kernels, finish(): pl.pallas_call(finish_kernel, grid=(span // TILE,), in_specs=[pl.BlockSpe...  5.05 us
  transfers between devices with their start and end apart: 18, of which 11 were waited for; matrix products, arithmetic and copies ran while one was open for 6% of the time, Pallas kernels for 42%

commit v1 on v0

v1 whole, which is shorter than its diff:
```python
import functools

import jax
import jax.numpy as jnp
from jax import lax
from jax.experimental import pallas as pl
from jax.experimental.pallas import tpu as pltpu
from jax.sharding import PartitionSpec as P

TILE = 512
RING = 4
VMEM = 60 * 1024 * 1024
ANY = pl.BlockSpec(memory_space=pl.ANY)


def swap(value, axis, size, mask):
    return lax.ppermute(value, axis, [(i, i ^ mask) for i in range(size)])


def split_kernel(first, grad_ref, *refs):
    me = lax.axis_index("dp")
    out_ref = refs[-1]
    blocks = [grad_ref[:, k, :] for k in range(grad_ref.shape[1])]
    bit = 1
    while bit < len(blocks):
        flip = (me & bit) != 0
        blocks = [jnp.where(flip, blocks[k ^ bit], blocks[k]) for k in range(len(blocks))]
        bit *= 2
    for k in range(out_ref.shape[0]):
        out_ref[k] = blocks[first + k].T


def split_blocks(out_grad, first, after):
    rows, n, width = out_grad.shape
    step = rows // 4
    return pl.pallas_call(
        functools.partial(split_kernel, first),
        grid=(4,),
        in_specs=[pl.BlockSpec((step, n, width), lambda i: (i, 0, 0))] + [ANY] * len(after),
        out_specs=pl.BlockSpec((n // 2, width, step), lambda i: (0, 0, i)),
        out_shape=jax.ShapeDtypeStruct((n // 2, width, rows), out_grad.dtype),
        compiler_params=pltpu.CompilerParams(vmem_limit_bytes=VMEM),
        name="split_blocks",
    )(out_grad, *after)


def gated(hidden, gate_ref, proj_ref):
    gate = gate_ref[...].T.astype(jnp.float32)
    silu = gate * (0.5 + 0.5 * jnp.tanh(0.5 * gate))
    up_grad = (hidden * silu).astype(jnp.bfloat16)
    return jnp.dot(proj_ref[...], up_grad, preferred_element_type=jnp.float32)


def project_kernel(tiles, ahead, pieces, chained, carried, shard_ref, *refs):
    refs = list(refs)
    take = lambda n: [refs.pop(0) for _ in range(n)]
    grads = take(pieces)
    weights = take(2 * pieces)
    gate_ref, proj_ref = take(2) if tiles else (None, None)
    (before_ref,) = take(1) if chained else (None,)
    (partial_ref,) = take(1) if carried else (None,)
    sum_ref, odd_ref, even_ref = [refs.pop() for _ in range(3)] if tiles else (None,) * 3
    later_ref = refs.pop() if ahead else None
    out_ref = refs.pop() if tiles else None
    step = pl.program_id(0)

    def multiply(hidden_ref):
        hidden = partial_ref[...] if carried else None
        for k, grad_ref in enumerate(grads):
            for p in range(2):
                term = jnp.dot(
                    weights[2 * k + p][...], grad_ref[p], preferred_element_type=jnp.float32
                )
                hidden = term if hidden is None else hidden + term
        hidden_ref[...] = hidden

    if not tiles:
        multiply(later_ref)
        return

    def reduce(hidden_ref):
        sum_ref[...] += gated(hidden_ref[...], gate_ref, proj_ref)

    @pl.when(step == 0)
    def _():
        sum_ref[...] = before_ref[...] if chained else jnp.zeros_like(sum_ref)
        multiply(even_ref)

    @pl.when((step > 0) & (step < tiles) & (lax.rem(step, 2) == 1))
    def _():
        reduce(even_ref)
        multiply(odd_ref)

    @pl.when((step > 0) & (step < tiles) & (lax.rem(step, 2) == 0))
    def _():
        reduce(odd_ref)
        multiply(even_ref)

    @pl.when(step == tiles)
    def _():
        reduce(even_ref if tiles % 2 else odd_ref)
        out_ref[...] = sum_ref[...]
        if ahead:
            multiply(later_ref)

    if ahead > 1:

        @pl.when(step > tiles)
        def _():
            multiply(later_ref)


def project(shard, grads, gate, weights, proj, offset, span, extra, gate_column, before, partial, after):
    places = [place for place, _ in grads]
    pieces = [piece for _, piece in grads]
    _, width, rows = pieces[0].shape
    count = weights[0].shape[1] // width
    k = proj.shape[0]
    tile = TILE if (span + extra) % TILE == 0 else span + extra
    tiles, ahead = span // tile, extra // tile
    first, gate_first = offset // tile, gate_column // tile
    now = lambda i: jnp.minimum(i, tiles + ahead - 1)
    last = lambda i: jnp.clip(i - 1, 0, max(tiles - 1, 0))
    chained, carried = before is not None, partial is not None
    total = pl.BlockSpec((k, rows), lambda i, s: (0, 0))
    later = pl.BlockSpec((tile, rows), lambda i, s: (jnp.maximum(i - tiles, 0), 0))

    def weight_spec(place):
        return pl.BlockSpec(
            (tile, width), lambda i, s: (first + now(i), lax.rem(s[0] + count - place, count))
        )

    specs = [pl.BlockSpec((2, width, rows), lambda i, s: (0, 0, 0)) for _ in pieces]
    specs += [weight_spec(place) for place in places for _ in range(2)]
    operands = pieces + [weight for _ in places for weight in weights]
    if tiles:
        specs += [
            pl.BlockSpec((rows, tile), lambda i, s: (0, gate_first + last(i))),
            pl.BlockSpec((k, tile), lambda i, s: (0, first + last(i))),
        ]
        operands += [gate, proj]
    if chained:
        specs.append(total)
        operands.append(before)
    if carried:
        specs.append(pl.BlockSpec((tile, rows), lambda i, s: (first + now(i), 0)))
        operands.append(partial)
    hidden = pltpu.VMEM((tile, rows), jnp.float32)
    depth = 2 * width * len(pieces)
    return pl.pallas_call(
        functools.partial(project_kernel, tiles, ahead, len(pieces), chained, carried),
        grid_spec=pltpu.PrefetchScalarGridSpec(
            num_scalar_prefetch=1,
            grid=(tiles + max(ahead, 1) if tiles else ahead,),
            in_specs=specs + [ANY] * len(after),
            out_specs=[total] * bool(tiles) + [later] * bool(ahead),
            scratch_shapes=[hidden, hidden, pltpu.VMEM((k, rows), jnp.float32)] if tiles else [],
        ),
        out_shape=[jax.ShapeDtypeStruct((k, rows), jnp.float32)] * bool(tiles)
        + [jax.ShapeDtypeStruct((extra, rows), jnp.float32)] * bool(ahead),
        compiler_params=pltpu.CompilerParams(vmem_limit_bytes=VMEM),
        cost_estimate=pl.CostEstimate(
            flops=2 * rows * (span + extra) * depth,
            bytes_accessed=2 * (span + extra) * (depth + rows),
            transcendentals=rows * span,
        ),
        name="project",
    )(shard, *operands, *after)


def finish_kernel(hidden_ref, gate_ref, proj_ref, before_ref, *refs):
    out_ref, sum_ref = refs[-2:]
    part = gated(hidden_ref[...], gate_ref, proj_ref)

    @pl.when(pl.program_id(0) == 0)
    def _():
        sum_ref[...] = before_ref[...] + part

    @pl.when(pl.program_id(0) > 0)
    def _():
        sum_ref[...] += part

    @pl.when(pl.program_id(0) == pl.num_programs(0) - 1)
    def _():
        out_ref[...] = sum_ref[...].astype(out_ref.dtype)


def finish(hidden, gate, proj, offset, before, dtype, after):
    span, rows = hidden.shape
    k = proj.shape[0]
    first = offset // TILE
    total = pl.BlockSpec((k, rows), lambda i: (0, 0))
    return pl.pallas_call(
        finish_kernel,
        grid=(span // TILE,),
        in_specs=[
            pl.BlockSpec((TILE, rows), lambda i: (i, 0)),
            pl.BlockSpec((rows, TILE), lambda i: (0, i)),
            pl.BlockSpec((k, TILE), lambda i: (0, first + i)),
            total,
        ]
        + [ANY] * len(after),
        out_specs=total,
        out_shape=jax.ShapeDtypeStruct((k, rows), dtype),
        scratch_shapes=[pltpu.VMEM((k, rows), jnp.float32)],
        compiler_params=pltpu.CompilerParams(vmem_limit_bytes=VMEM),
        name="finish",
    )(hidden, gate, proj, before, *after)


def score_kernel(n_both, parts, out_ref):
    *parts, query_ref = parts
    total = lambda refs: functools.reduce(jnp.add, [ref[...].astype(jnp.float32) for ref in refs])
    grad = total(parts[n_both:])
    inputs, own = jnp.split(total(parts[:n_both]), 2)
    grad += own
    high = grad.astype(jnp.bfloat16)
    low = (grad - high.astype(jnp.float32)).astype(jnp.bfloat16)
    both = jnp.concatenate([high, low], axis=0)
    count = out_ref.shape[0]
    k = inputs.shape[0]
    group = 8
    scores = jnp.zeros(out_ref.shape, jnp.float32)
    for i in range(0, k, group):
        part = jnp.dot(
            query_ref[i * count : (i + group) * count, :], both, preferred_element_type=jnp.float32
        )
        for n in range(group):
            scores += inputs[i + n : i + n + 1, :] * part[n * count : (n + 1) * count, :]
    out_ref[...] = scores


def pair_queries(queries, k):
    pairs = queries.reshape(queries.shape[0], k, k).transpose(1, 0, 2).reshape(-1, k)
    return jnp.concatenate([pairs, pairs], axis=1)


def score(both, grads, pairs):
    k, rows = grads[0].shape
    return pl.pallas_call(
        lambda *refs: score_kernel(len(both), refs[:-1], refs[-1]),
        out_shape=jax.ShapeDtypeStruct((pairs.shape[0] // k, rows), jnp.float32),
        compiler_params=pltpu.CompilerParams(vmem_limit_bytes=VMEM),
        name="score",
    )(*both, *grads, pairs)


def chunks_of(hidden):
    units = hidden // TILE
    last = 3 * TILE if hidden % TILE == 0 and units >= 8 else 0
    return hidden - last, last


def on_device(n_dp, n_tensor, inputs, out_grad, gate_pre, down_weight, proj_in, proj_out, queries):
    rows = out_grad.shape[0]
    hidden = gate_pre.shape[1]
    me = lax.axis_index("dp")
    shard = lax.axis_index("tensor").astype(jnp.int32).reshape(1)
    far, near = n_dp // 2, 1
    ring = n_tensor <= RING
    main, extra = chunks_of(hidden)

    def onward(piece, hold=None):
        if hold is not None:
            piece, _ = lax.optimization_barrier((piece, hold))
        return lax.ppermute(piece, "tensor", [(i, (i + 1) % n_tensor) for i in range(n_tensor)])

    def gather(block):
        grad = lax.all_gather(block, "tensor", axis=0, tiled=False)
        return jnp.transpose(grad, (1, 0, 2, 3)).reshape(2, -1, rows)

    def spread(value, mask):
        if not ring:
            total = lax.psum(value.astype(jnp.float32), "tensor")
            return [swap(total, "dp", n_dp, mask) if mask else total]
        got = [value] if not mask else []
        for step in range(0 if mask else 1, n_tensor):
            pairs = [
                (z * n_dp + d, (z + step) % n_tensor * n_dp + (d ^ mask))
                for z in range(n_tensor)
                for d in range(n_dp)
            ]
            got.append(lax.ppermute(value, ("tensor", "dp"), pairs))
        return got

    weights = (down_weight, swap(down_weight, "dp", n_dp, near))
    far_query = swap(queries, "dp", n_dp, far)

    own_blocks = split_blocks(out_grad, 0, ())
    far_blocks = split_blocks(out_grad, n_dp // 2, (own_blocks,))
    far_blocks, _ = lax.optimization_barrier((far_blocks, far_query))
    far_start = swap(far_blocks, "dp", n_dp, far)
    own = [own_blocks, onward(own_blocks)] if ring and n_tensor > 1 else [own_blocks]
    gates, far_start, own[-1] = lax.optimization_barrier(
        ((gate_pre[:, :main], gate_pre[:, main:]), far_start, own[-1])
    )
    far_gate, last_gate = (swap(part, "dp", n_dp, far) if part.size else None for part in gates)

    def all_pairs(hold):
        blocks, _ = lax.optimization_barrier(((queries, far_query), hold))
        blocks += tuple(swap(block, "dp", n_dp, near) for block in blocks)
        width = queries.shape[1]
        merged = jnp.zeros((queries.shape[0], n_dp * width), queries.dtype)
        for mask, block in zip((0, far, near, far ^ near), blocks):
            merged = lax.dynamic_update_slice(merged, block, (0, (me ^ mask) * width))
        return pair_queries(merged, proj_in.shape[1])

    proj_out = proj_out.T
    if ring and n_tensor > 1:
        split = n_tensor // 2
        while len(own) <= split:
            own.append(onward(own[-1]))
        own_early = list(enumerate(own))[:split]
        (own_sum,) = project(
            shard, own_early, gate_pre, weights, proj_out, 0, hidden, 0, 0, None, None, ()
        )
        early_sum = own_sum
        pairs = all_pairs(early_sum)
        others = [far_start]
        for _ in range(split - 1):
            others.append(onward(others[-1]))
        far_early = list(enumerate(others))
        (partial,) = project(
            shard, far_early, None, weights, proj_out, 0, 0, hidden, 0, None, None, (own_sum,)
        )
        while len(own) < n_tensor:
            own.append(onward(own[-1], early_sum))
        own_late = list(enumerate(own))[split:]
        middle = hidden // 2 if hidden % (2 * TILE) == 0 else hidden
        after = (partial,)
        for s in range(0, hidden, middle):
            (own_sum,) = project(
                shard, own_late, gate_pre, weights, proj_out, s, middle, 0, s, own_sum, None, after
            )
            if s == 0:
                while len(others) < n_tensor:
                    hold = own_sum if len(others) == n_tensor - 1 else early_sum
                    others.append(onward(others[-1], hold))
            after = (pairs,)
        far_late = list(enumerate(others))[split:]
    else:
        (own_sum,) = project(
            shard, [(0, gather(own_blocks))], gate_pre, weights, proj_out, 0, hidden, 0, 0, None, None, ()
        )
        far_late, partial = [(0, gather(far_start))], None
        pairs = all_pairs(own_sum)

    input_part = lax.dot_general(
        proj_in, inputs, (((0,), (1,)), ((), ())), preferred_element_type=jnp.float32
    )
    both = jnp.concatenate([input_part, own_sum])
    places = [place for place, _ in far_late]
    both, far_gate, pieces = lax.optimization_barrier((both, far_gate, [p for _, p in far_late]))
    far_late = list(zip(places, pieces))
    terms = spread(both, 0)

    far_sum, *later = project(
        shard, far_late, far_gate, weights, proj_out, 0, main, extra, 0, None, partial, (both,)
    )
    if extra:
        far_sum = finish(later[0], last_gate, proj_out, main, far_sum, jnp.bfloat16, ())
    return score(terms, spread(far_sum, far), pairs)


def solution(mesh):
    return jax.shard_map(
        functools.partial(on_device, mesh.shape["dp"], mesh.shape["tensor"]),
        mesh=mesh,
        in_specs=(
            P(("parts", "dp"), "tensor"),
            P(("parts", "dp"), None, "tensor"),
            P(("parts", "dp"), "tensor"),
            P("tensor", "dp"),
            P("tensor", None),
            P("tensor", None),
            P("tensor", "dp"),
        ),
        out_specs=P("tensor", ("parts", "dp")),
        check_vma=False,
    )
```

time: 251 us -> 227 us (0.904)
  waiting for transfers between devices: 105 us -> 51 us
  Pallas kernels: 113 us -> 133 us
  starting transfers between devices: 15.8 us -> 22.1 us
  local copies, waits for them, and re-layouts: 12.8 us -> 15.7 us
    ppermute x6 -> x13, waiting for transfers between devices: 76.2 us -> 37.9 us  [the longest x6 30.7 us: onward(): lax.ppermute(piece, 'tensor', [(i, (i + 1) % n_tensor) for i in range(n_t...]
    pallas_call x4 -> x6, Pallas kernels: 97.4 us -> 117 us  [the longest x5 113 us: project(): pl.pallas_call(functools.partial(project_kernel, tiles, ahead, len(pieces...]
    ppermute x12 -> x7, waiting for transfers between devices: 29.1 us -> 13.1 us  [swap(): return lax.ppermute(value, axis, [(i, i ^ mask) for i in range(size)])]
    ppermute x6 -> x13, starting transfers between devices: 3.12 us -> 16.3 us  [the longest x7 10.2 us: spread(): got.append(lax.ppermute(value, ('tensor', 'dp'), pairs))]
    ppermute x12 -> x7, starting transfers between devices: 12.7 us -> 5.77 us  [swap(): return lax.ppermute(value, axis, [(i, i ^ mask) for i in range(size)])]
  transfers between devices with their start and end apart: 18 -> 20, of which waited for: 11 -> 10; matrix products, arithmetic and copies ran while one was open for 6% -> 7% of each run, Pallas kernels for 42% -> 57%
where the time goes in v1:
time: 227 us; the launch traced here: 226 us
  Pallas kernels  133 us (59%)
  waiting for transfers between devices  51 us (22%)
  starting transfers between devices  22.1 us (10%)
  local copies, waits for them, and re-layouts  15.7 us (7%)
  other arithmetic  2.48 us (1%)
    pallas_call x5, Pallas kernels, project(): pl.pallas_call(functools.partial(project_kernel, tiles, ahead, len(pieces...  113 us
    ppermute x6, waiting for transfers between devices, onward(): lax.ppermute(piece, 'tensor', [(i, (i + 1) % n_tensor) for i in range(n_t...  30.7 us
    ppermute x7, waiting for transfers between devices, swap(): return lax.ppermute(value, axis, [(i, i ^ mask) for i in range(size)])  13.1 us
    pallas_call x2, Pallas kernels, split_blocks(): pl.pallas_call(functools.partial(split_kernel, first), grid=(4,), in_spec...  10.8 us
    ppermute x7, starting transfers between devices, spread(): got.append(lax.ppermute(value, ('tensor', 'dp'), pairs))  10.2 us
    ppermute x7, waiting for transfers between devices, spread(): got.append(lax.ppermute(value, ('tensor', 'dp'), pairs))  7.24 us
    ppermute x6, starting transfers between devices, onward(): lax.ppermute(piece, 'tensor', [(i, (i + 1) % n_tensor) for i in range(n_t...  6.09 us
    ppermute x7, starting transfers between devices, swap(): return lax.ppermute(value, axis, [(i, i ^ mask) for i in range(size)])  5.77 us
  transfers between devices with their start and end apart: 20, of which 10 were waited for; matrix products, arithmetic and copies ran while one was open for 7% of the time, Pallas kernels for 57%

profile of v1, /device:TPU:0, one launch (start us, length us, event | category | flops | bytes accessed | tf_op | source)
XLA Modules:
  0.0 225.6 jit_solution(599223082331402373)
XLA Ops:
  0.0 0.0 copy-start
  0.0 0.5 collective-permute-start.4
  0.5 2.6 %collective-permute-start = (bf16[64,1024]{1,0:T(8,128)(2,1)}, bf16[64,1024]{1,0:T(8,128)(2,1)S(1)}, u32[]{:S(2)}, u32[]{:S(2)}) collective-permute-start(bf16[64,1024]{1,0:T(8,128)(2,1)} %param.13), channel_id=1, source_target_pairs={{0,2},{1,3},{2,0},{3,1},{4,6},{5,7},{6,4},{7,5},{8,10},{9,11},{10,... | collective-permute-start | bytes 393224 | tf_op jit(solution)/shard_map/ppermute | solution.py:17
  3.0 5.4 %split_blocks.2.refs_0_ = bf16[2,512,512]{2,1,0:T(8,128)(2,1)} custom-call(bf16[512,4,512]{2,1,0:T(4,128)(2,1)} %grad_ref.3), custom_call_target="tpu_custom_call" | custom-call | tf_op jit(solution)/shard_map/split_blocks/pallas_call | solution.py:36
  8.4 1.6 collective-permute-start.2
  10.0 5.4 %split_blocks.3 = bf16[2,512,512]{2,1,0:T(8,128)(2,1)} custom-call(bf16[512,4,512]{2,1,0:T(4,128)(2,1)} %grad_ref.3, bf16[2,512,512]{2,1,0:T(8,128)(2,1)} %split_blocks.2.refs_0_), custom_call_target="tpu_custom_call" | custom-call | tf_op jit(solution)/shard_map/split_blocks/pallas_call | solution.py:36
  15.3 0.0 collective-permute-done
  15.3 0.6 collective-permute-start.1
  15.9 2.7 %slice.7 = bf16[512,1536]{1,0:T(8,128)(2,1)} slice(bf16[512,7168]{1,0:T(8,128)(2,1)} %refs_6_.5), slice={[0:512], [5632:7168]} | slice | bytes 3145728 | tf_op jit(solution)/shard_map/slice | solution.py:295
  18.6 5.5 %slice.6 = bf16[512,5632]{1,0:T(8,128)(2,1)} slice(bf16[512,7168]{1,0:T(8,128)(2,1)} %refs_6_.5), slice={[0:512], [0:5632]} | slice | bytes 11534336 | tf_op jit(solution)/shard_map/slice | solution.py:295
  24.1 11.7 %collective-permute-done.2.refs_1_ = bf16[2,512,512]{2,1,0:T(8,128)(2,1)} collective-permute-done((bf16[2,512,512]{2,1,0:T(8,128)(2,1)}, bf16[2,512,512]{2,1,0:T(8,128)(2,1)}, u32[]{:S(2)}, u32[]{:S(2)}) %collective-permute-start.2) | collective-permute-done | bytes 1048608 | tf_op jit(solution)/shard_map/ppermute | solution.py:266
  35.8 4.7 %collective-permute-done.1.refs_0_ = bf16[2,512,512]{2,1,0:T(8,128)(2,1)S(1)} collective-permute-done((bf16[2,512,512]{2,1,0:T(8,128)(2,1)}, bf16[2,512,512]{2,1,0:T(8,128)(2,1)S(1)}, u32[]{:S(2)}, u32[]{:S(2)}) %collective-permute-start.1) | collective-permute-done | bytes 1048608 | tf_op jit(solution)/shard_map/ppermute | solution.py:17
  40.5 0.5 collective-permute-start.9
  41.0 1.4 fusion
  42.5 1.6 collective-permute-start.3
  44.0 1.6 collective-permute-start.6
  45.6 0.0 collective-permute-done.4.refs_3_.refs_5_
  45.6 27.3 %project.5.refs_6_.refs_8_ = f32[64,512]{1,0:T(8,128)} custom-call(s32[1]{0:T(128)} %bitcast.shard_ref, bf16[2,512,512]{2,1,0:T(8,128)(2,1)} %split_blocks.2.refs_0_, bf16[2,512,512]{2,1,0:T(8,128)(2,1)} %collective-permute-done.2.refs_1_, bf16[7168,2048]{1,0:T(8,128)(2,1)} %refs_4_.9, bf16[7168,2048]{1,0:T(8,128)(2,1)} %collective-permute-done.4.refs_3_.refs_5_, ...), custom_call_target="tpu_custom_call" | custom-call | flops 15032385536 | bytes 36700160 | tf_op jit(solution)/shard_map/project/pallas_call | solution.py:150
  72.9 17.8 %collective-permute-done.6.refs_1_ = bf16[2,512,512]{2,1,0:T(8,128)(2,1)S(1)} collective-permute-done((bf16[2,512,512]{2,1,0:T(8,128)(2,1)S(1)}, bf16[2,512,512]{2,1,0:T(8,128)(2,1)S(1)}, u32[]{:S(2)}, u32[]{:S(2)}) %collective-permute-start.6) | collective-permute-done | bytes 1048608 | tf_op jit(solution)/shard_map/ppermute | solution.py:266
  90.7 0.0 collective-permute-done.3.refs_0_
  90.7 0.1 collective-permute-start.7
  90.8 0.9 copy-done.6
  91.7 0.0 collective-permute-start.8
  91.7 0.0 collective-permute-start.5
  91.7 1.4 collective-permute-start.10
  93.0 25.6 %project.6.refs_9_.refs_8_ = f32[7168,512]{1,0:T(8,128)} custom-call(s32[1]{0:T(128)} %bitcast.shard_ref, bf16[2,512,512]{2,1,0:T(8,128)(2,1)} %copy-done.5, bf16[2,512,512]{2,1,0:T(8,128)(2,1)} %copy-done.6, bf16[7168,2048]{1,0:T(8,128)(2,1)} %refs_4_.9, bf16[7168,2048]{1,0:T(8,128)(2,1)} %collective-permute-done.4.refs_3_.refs_5_, ...), custom_call_target="tpu_custom_call" | custom-call | flops 15032385536 | bytes 36700160 | tf_op jit(solution)/shard_map/project/pallas_call | solution.py:150
  118.7 0.0 collective-permute-done.7
  118.7 1.6 collective-permute-start.15
  120.3 0.0 collective-permute-done.8
  120.3 2.1 reshape.10
  122.5 1.9 copy.8
  124.4 0.0 collective-permute-done.5.refs_1_
  124.4 1.0 copy-done.3
  125.4 15.5 %project.7.refs_8_ = f32[64,512]{1,0:T(8,128)} custom-call(s32[1]{0:T(128)} %bitcast.shard_ref, bf16[2,512,512]{2,1,0:T(8,128)(2,1)} %copy-done.2, bf16[2,512,512]{2,1,0:T(8,128)(2,1)} %copy-done.3, bf16[7168,2048]{1,0:T(8,128)(2,1)} %refs_4_.9, bf16[7168,2048]{1,0:T(8,128)(2,1)} %collective-permute-done.4.refs_3_.refs_5_, bf16[7168,2048]{1,0:T(8,128)(2,1)} %refs_4_.9, ...), custom_call_target="tpu_custom_call" | custom-call | flops 7516192768 | bytes 18350080 | tf_op jit(solution)/shard_map/project/pallas_call | solution.py:150
  140.8 0.8 collective-permute-done.10.refs_0_
  141.6 0.0 collective-permute-start.11
  141.6 1.6 pad_maximum_fusion.refs_9_.refs_8_
  143.2 15.5 %project.8 = f32[64,512]{1,0:T(8,128)} custom-call(s32[1]{0:T(128)} %bitcast.shard_ref, bf16[2,512,512]{2,1,0:T(8,128)(2,1)} %copy-done.2, bf16[2,512,512]{2,1,0:T(8,128)(2,1)} %copy-done.3, bf16[7168,2048]{1,0:T(8,128)(2,1)} %refs_4_.9, bf16[7168,2048]{1,0:T(8,128)(2,1)} %collective-permute-done.4.refs_3_.refs_5_, bf16[7168,2048]{1,0:T(8,128)(2,1)} %refs_4_.9, ...), custom_call_target="tpu_custom_call" | custom-call | flops 7516192768 | bytes 18350080 | tf_op jit(solution)/shard_map/project/pallas_call | solution.py:150
  158.7 0.9 pad_maximum_fusion.1.refs_9_.refs_0_
  159.6 8.4 %collective-permute-done.9.refs_6_ = bf16[512,5632]{1,0:T(8,128)(2,1)} collective-permute-done((bf16[512,5632]{1,0:T(8,128)(2,1)}, bf16[512,5632]{1,0:T(8,128)(2,1)}, u32[]{:S(2)}, u32[]{:S(2)}) %collective-permute-start.9) | collective-permute-done | bytes 5767200 | tf_op jit(solution)/shard_map/ppermute | solution.py:17
  168.0 0.4 collective-permute-done.11.refs_1_
  168.4 1.9 collective-permute-start.14
  170.4 0.7 collective-permute-start.13
  171.1 1.6 collective-permute-start.12
  172.7 29.5 %project.9 = (f32[64,512]{1,0:T(8,128)}, f32[1536,512]{1,0:T(8,128)}) custom-call(s32[1]{0:T(128)} %bitcast.shard_ref, bf16[2,512,512]{2,1,0:T(8,128)(2,1)} %collective-permute-done.10.refs_0_, bf16[2,512,512]{2,1,0:T(8,128)(2,1)} %copy-done.7, bf16[7168,2048]{1,0:T(8,128)(2,1)} %refs_4_.9, bf16[7168,2048]{1,0:T(8,128)(2,1)} %collective-permute-done.4.refs_3_.refs_5_, ...), custom_call_target="tpu_custom_call" | custom-call | flops 15032385536 | bytes 36700160 | tf_op jit(solution)/shard_map/project/pallas_call | solution.py:150
  202.2 0.0 collective-permute-done.15.gate_ref
  202.2 0.0 copy-start.1
  202.2 5.1 %finish.1 = bf16[64,512]{1,0:T(8,128)(2,1)} custom-call(f32[1536,512]{1,0:T(8,128)} %get-tuple-element.34.hidden_ref, bf16[512,1536]{1,0:T(8,128)(2,1)} %collective-permute-done.15.gate_ref, bf16[64,7168]{1,0:T(8,128)(2,1)} %bitcast.10, f32[64,512]{1,0:T(8,128)} %get-tuple-element.36.before_ref), custom_call_target="tpu_custom_call" | custom-call | tf_op jit(solution)/shard_map/finish/pallas_call | solution.py:193
  207.2 2.2 collective-permute-start.19
  209.4 1.3 collective-permute-start.18
  210.7 1.9 collective-permute-done.19.refs_7_
  212.6 1.2 collective-permute-start.17
  213.8 2.0 collective-permute-done.18.refs_6_
  215.8 1.3 collective-permute-start.16
  217.2 2.6 %collective-permute-done.17.refs_5_ = bf16[64,512]{1,0:T(8,128)(2,1)S(1)} collective-permute-done((bf16[64,512]{1,0:T(8,128)(2,1)}, bf16[64,512]{1,0:T(8,128)(2,1)S(1)}, u32[]{:S(2)}, u32[]{:S(2)}) %collective-permute-start.17) | collective-permute-done | bytes 65568 | tf_op jit(solution)/shard_map/ppermute | solution.py:283
  219.8 0.7 collective-permute-done.16.refs_4_
  220.5 0.0 collective-permute-done.14.refs_3_
  220.5 0.0 collective-permute-done.13.refs_2_
  220.5 0.0 collective-permute-done.12.refs_1_
  220.6 0.6 copy-done.17
  221.1 0.1 copy-done.10
  221.2 0.1 copy-done.11
  221.3 0.7 copy-done.12
  222.0 3.6 %score.1 = f32[64,512]{1,0:T(8,128)} custom-call(f32[128,512]{1,0:T(8,128)} %copy-done.4, f32[128,512]{1,0:T(8,128)} %copy-done.12, f32[128,512]{1,0:T(8,128)} %copy-done.11, f32[128,512]{1,0:T(8,128)} %copy-done.10, bf16[64,512]{1,0:T(8,128)(2,1)} %copy-done.17, bf16[64,512]{1,0:T(8,128)(2,1)} %copy-done.16, bf16[64,512]{1,0:T(8,128)(2,1)} %copy-done.15, ...), custom_call_target="tpu_custom_call" | custom-call | tf_op jit(solution)/shard_map/score/pallas_call | solution.py:240
  (33 shorter events, 0.2 us)
Async XLA Ops:
  0.0 41.0 %copy-start = (bf16[512,2048]{1,0:T(8,128)(2,1)S(1)}, bf16[512,2048]{1,0:T(8,128)(2,1)}, u32[]{:S(2)}) copy-start(bf16[512,2048]{1,0:T(8,128)(2,1)} %param.7) | copy-start | bytes 6291460
  0.0 45.6 %collective-permute-start.4 = (bf16[7168,2048]{1,0:T(8,128)(2,1)}, bf16[7168,2048]{1,0:T(8,128)(2,1)}, u32[]{:S(2)}, u32[]{:S(2)}) collective-permute-start(bf16[7168,2048]{1,0:T(8,128)(2,1)} %refs_4_.9), channel_id=1, source_target_pairs={{0,1},{1,0},{2,3},{3,2},{4,5},{5,4},{6,7},{7,6},{8,9},{9,8},{10,11... | collective-permute-start | bytes 88080392 | tf_op jit(solution)/shard_map/ppermute | solution.py:17
  0.5 14.9 %collective-permute-start = (bf16[64,1024]{1,0:T(8,128)(2,1)}, bf16[64,1024]{1,0:T(8,128)(2,1)S(1)}, u32[]{:S(2)}, u32[]{:S(2)}) collective-permute-start(bf16[64,1024]{1,0:T(8,128)(2,1)} %param.13), channel_id=1, source_target_pairs={{0,2},{1,3},{2,0},{3,1},{4,6},{5,7},{6,4},{7,5},{8,10},{9,11},{10,... | collective-permute-start | bytes 393224 | tf_op jit(solution)/shard_map/ppermute | solution.py:17
  8.4 27.4 %collective-permute-start.2 = (bf16[2,512,512]{2,1,0:T(8,128)(2,1)}, bf16[2,512,512]{2,1,0:T(8,128)(2,1)}, u32[]{:S(2)}, u32[]{:S(2)}) collective-permute-start(bf16[2,512,512]{2,1,0:T(8,128)(2,1)} %split_blocks.2.refs_0_), channel_id=1, source_target_pairs={{0,4},{4,8},{8,12},{12,0},{1,5},{5,9},{9,13},{13,1},{2,6},{6,10},{... | collective-permute-start | bytes 3145736 | tf_op jit(solution)/shard_map/ppermute | solution.py:266
  15.3 25.2 %collective-permute-start.1 = (bf16[2,512,512]{2,1,0:T(8,128)(2,1)}, bf16[2,512,512]{2,1,0:T(8,128)(2,1)S(1)}, u32[]{:S(2)}, u32[]{:S(2)}) collective-permute-start(bf16[2,512,512]{2,1,0:T(8,128)(2,1)} %split_blocks.3), channel_id=1, source_target_pairs={{0,2},{1,3},{2,0},{3,1},{4,6},{5,7},{6,4},{7,5},{8,10},{9,11},{10,... | collective-permute-start | bytes 3145736 | tf_op jit(solution)/shard_map/ppermute | solution.py:17
  18.6 22.5 %copy-start.9 = (bf16[2048,64]{0,1:T(8,128)(2,1)S(1)}, bf16[2048,64]{0,1:T(8,128)(2,1)}, u32[]{:S(2)}) copy-start(bf16[2048,64]{0,1:T(8,128)(2,1)} %param.11) | copy-start | bytes 786436
  40.5 32.4 %copy-start.5 = (bf16[2,512,512]{2,1,0:T(8,128)(2,1)}, bf16[2,512,512]{2,1,0:T(8,128)(2,1)S(1)}, u32[]{:S(2)}) copy-start(bf16[2,512,512]{2,1,0:T(8,128)(2,1)S(1)} %collective-permute-done.1.refs_0_) | copy-start | bytes 3145732
  40.5 127.5 %collective-permute-start.9 = (bf16[512,5632]{1,0:T(8,128)(2,1)}, bf16[512,5632]{1,0:T(8,128)(2,1)}, u32[]{:S(2)}, u32[]{:S(2)}) collective-permute-start(bf16[512,5632]{1,0:T(8,128)(2,1)} %slice.6), channel_id=1, source_target_pairs={{0,2},{1,3},{2,0},{3,1},{4,6},{5,7},{6,4},{7,5},{8,10},{9,11},{10,... | collective-permute-start | bytes 17301512 | tf_op jit(solution)/shard_map/ppermute | solution.py:17
  42.5 48.2 %collective-permute-start.3 = (bf16[2,512,512]{2,1,0:T(8,128)(2,1)}, bf16[2,512,512]{2,1,0:T(8,128)(2,1)S(1)}, u32[]{:S(2)}, u32[]{:S(2)}) collective-permute-start(bf16[2,512,512]{2,1,0:T(8,128)(2,1)} %collective-permute-done.2.refs_1_), channel_id=1, source_target_pairs={{0,4},{4,8},{8,12},{12,0},{1,5},{5,9},{9,13},{13,1},{2,6},{6,10},{... | collective-permute-start | bytes 3145736 | tf_op jit(solution)/shard_map/ppermute | solution.py:266
  44.0 46.7 %collective-permute-start.6 = (bf16[2,512,512]{2,1,0:T(8,128)(2,1)S(1)}, bf16[2,512,512]{2,1,0:T(8,128)(2,1)S(1)}, u32[]{:S(2)}, u32[]{:S(2)}) collective-permute-start(bf16[2,512,512]{2,1,0:T(8,128)(2,1)S(1)} %collective-permute-done.1.refs_0_), channel_id=1, source_target_pairs={{0,4},{4,8},{8,12},{12,0},{1,5},{5,9},{9,13},{13,1},{2,6},{6,10},{... | collective-permute-start | bytes 3145736 | tf_op jit(solution)/shard_map/ppermute | solution.py:266
  45.6 45.1 %copy-start.13 = (bf16[64,1024]{1,0:T(8,128)(2,1)S(1)}, bf16[64,1024]{1,0:T(8,128)(2,1)}, u32[]{:S(2)}) copy-start(bf16[64,1024]{1,0:T(8,128)(2,1)} %param.13) | copy-start | bytes 393220
  90.7 1.0 copy-start.6
  90.7 27.9 %copy-start.2 = (bf16[2,512,512]{2,1,0:T(8,128)(2,1)}, bf16[2,512,512]{2,1,0:T(8,128)(2,1)S(1)}, u32[]{:S(2)}) copy-start(bf16[2,512,512]{2,1,0:T(8,128)(2,1)S(1)} %collective-permute-done.3.refs_0_) | copy-start | bytes 3145732
  90.7 28.0 %collective-permute-start.7 = (bf16[64,1024]{1,0:T(8,128)(2,1)S(1)}, bf16[64,1024]{1,0:T(8,128)(2,1)S(1)}, u32[]{:S(2)}, u32[]{:S(2)}) collective-permute-start(bf16[64,1024]{1,0:T(8,128)(2,1)S(1)} %copy-done.13), channel_id=1, source_target_pairs={{0,1},{1,0},{2,3},{3,2},{4,5},{5,4},{6,7},{7,6},{8,9},{9,8},{10,11... | collective-permute-start | bytes 393224 | tf_op jit(solution)/shard_map/ppermute | solution.py:17
  91.7 28.6 %collective-permute-start.8 = (bf16[64,1024]{1,0:T(8,128)(2,1)S(1)}, bf16[64,1024]{1,0:T(8,128)(2,1)S(1)}, u32[]{:S(2)}, u32[]{:S(2)}) collective-permute-start(bf16[64,1024]{1,0:T(8,128)(2,1)S(1)} %collective-permute-done), channel_id=1, source_target_pairs={{0,1},{1,0},{2,3},{3,2},{4,5},{5,4},{6,7},{7,6},{8,9},{9,8},{10,11... | collective-permute-start | bytes 393224 | tf_op jit(solution)/shard_map/ppermute | solution.py:17
  91.7 32.7 %collective-permute-start.5 = (bf16[2,512,512]{2,1,0:T(8,128)(2,1)S(1)}, bf16[2,512,512]{2,1,0:T(8,128)(2,1)S(1)}, u32[]{:S(2)}, u32[]{:S(2)}) collective-permute-start(bf16[2,512,512]{2,1,0:T(8,128)(2,1)S(1)} %collective-permute-done.3.refs_0_), channel_id=1, source_target_pairs={{0,4},{4,8},{8,12},{12,0},{1,5},{5,9},{9,13},{13,1},{2,6},{6,10},{... | collective-permute-start | bytes 3145736 | tf_op jit(solution)/shard_map/ppermute | solution.py:266
  91.7 49.9 %collective-permute-start.10 = (bf16[2,512,512]{2,1,0:T(8,128)(2,1)}, bf16[2,512,512]{2,1,0:T(8,128)(2,1)}, u32[]{:S(2)}, u32[]{:S(2)}) collective-permute-start(bf16[2,512,512]{2,1,0:T(8,128)(2,1)} %copy-done.6), channel_id=1, source_target_pairs={{0,4},{4,8},{8,12},{12,0},{1,5},{5,9},{9,13},{13,1},{2,6},{6,10},{... | collective-permute-start | bytes 3145736 | tf_op jit(solution)/shard_map/ppermute | solution.py:266
  118.7 83.5 %collective-permute-start.15 = (bf16[512,1536]{1,0:T(8,128)(2,1)}, bf16[512,1536]{1,0:T(8,128)(2,1)}, u32[]{:S(2)}, u32[]{:S(2)}) collective-permute-start(bf16[512,1536]{1,0:T(8,128)(2,1)} %slice.7), channel_id=1, source_target_pairs={{0,2},{1,3},{2,0},{3,1},{4,6},{5,7},{6,4},{7,5},{8,10},{9,11},{10,... | collective-permute-start | bytes 4718600 | tf_op jit(solution)/shard_map/ppermute | solution.py:17
  124.4 1.0 copy-start.3
  141.6 26.8 %collective-permute-start.11 = (bf16[2,512,512]{2,1,0:T(8,128)(2,1)}, bf16[2,512,512]{2,1,0:T(8,128)(2,1)S(1)}, u32[]{:S(2)}, u32[]{:S(2)}) collective-permute-start(bf16[2,512,512]{2,1,0:T(8,128)(2,1)} %collective-permute-done.10.refs_0_), channel_id=1, source_target_pairs={{0,4},{4,8},{8,12},{12,0},{1,5},{5,9},{9,13},{13,1},{2,6},{6,10},{... | collective-permute-start | bytes 3145736 | tf_op jit(solution)/shard_map/ppermute | solution.py:266
  143.2 15.5 %copy-start.8 = (f32[64,512]{1,0:T(8,128)S(1)}, f32[64,512]{1,0:T(8,128)}, u32[]{:S(2)}) copy-start(f32[64,512]{1,0:T(8,128)} %fusion) | copy-start | bytes 393220
  159.6 13.0 %copy-start.4 = (f32[128,512]{1,0:T(8,128)}, f32[128,512]{1,0:T(8,128)S(1)}, u32[]{:S(2)}) copy-start(f32[128,512]{1,0:T(8,128)S(1)} %pad_maximum_fusion.1.refs_9_.refs_0_) | copy-start | bytes 786436
  168.4 4.2 %copy-start.7 = (bf16[2,512,512]{2,1,0:T(8,128)(2,1)}, bf16[2,512,512]{2,1,0:T(8,128)(2,1)S(1)}, u32[]{:S(2)}) copy-start(bf16[2,512,512]{2,1,0:T(8,128)(2,1)S(1)} %collective-permute-done.11.refs_1_) | copy-start | bytes 3145732
  168.4 52.1 %collective-permute-start.14 = (f32[128,512]{1,0:T(8,128)S(1)}, f32[128,512]{1,0:T(8,128)S(1)}, u32[]{:S(2)}, u32[]{:S(2)}) collective-permute-start(f32[128,512]{1,0:T(8,128)S(1)} %pad_maximum_fusion.1.refs_9_.refs_0_), channel_id=1, source_target_pairs={{0,12},{1,13},{2,14},{3,15},{4,0},{5,1},{6,2},{7,3},{8,4},{9,5},{1... | collective-permute-start | bytes 786440 | tf_op jit(solution)/shard_map/ppermute | solution.py:283
  170.4 50.1 %collective-permute-start.13 = (f32[128,512]{1,0:T(8,128)S(1)}, f32[128,512]{1,0:T(8,128)S(1)}, u32[]{:S(2)}, u32[]{:S(2)}) collective-permute-start(f32[128,512]{1,0:T(8,128)S(1)} %pad_maximum_fusion.1.refs_9_.refs_0_), channel_id=1, source_target_pairs={{0,8},{1,9},{2,10},{3,11},{4,12},{5,13},{6,14},{7,15},{8,0},{9,1},... | collective-permute-start | bytes 786440 | tf_op jit(solution)/shard_map/ppermute | solution.py:283
  171.1 49.4 %collective-permute-start.12 = (f32[128,512]{1,0:T(8,128)S(1)}, f32[128,512]{1,0:T(8,128)S(1)}, u32[]{:S(2)}, u32[]{:S(2)}) collective-permute-start(f32[128,512]{1,0:T(8,128)S(1)} %pad_maximum_fusion.1.refs_9_.refs_0_), channel_id=1, source_target_pairs={{0,4},{1,5},{2,6},{3,7},{4,8},{5,9},{6,10},{7,11},{8,12},{9,13},{1... | collective-permute-start | bytes 786440 | tf_op jit(solution)/shard_map/ppermute | solution.py:283
  202.2 23.4 %copy-start.1 = (bf16[512,2048]{1,0:T(8,128)(2,1)S(1)}, bf16[512,2048]{1,0:T(8,128)(2,1)}, u32[]{:S(2)}) copy-start(bf16[512,2048]{1,0:T(8,128)(2,1)} %param.7) | copy-start | bytes 6291460
  207.2 5.4 %collective-permute-start.19 = (bf16[64,512]{1,0:T(8,128)(2,1)}, bf16[64,512]{1,0:T(8,128)(2,1)S(1)}, u32[]{:S(2)}, u32[]{:S(2)}) collective-permute-start(bf16[64,512]{1,0:T(8,128)(2,1)} %finish.1), channel_id=1, source_target_pairs={{0,14},{1,15},{2,12},{3,13},{4,2},{5,3},{6,0},{7,1},{8,6},{9,7},{1... | collective-permute-start | bytes 196616 | tf_op jit(solution)/shard_map/ppermute | solution.py:283
  209.4 6.4 %collective-permute-start.18 = (bf16[64,512]{1,0:T(8,128)(2,1)}, bf16[64,512]{1,0:T(8,128)(2,1)S(1)}, u32[]{:S(2)}, u32[]{:S(2)}) collective-permute-start(bf16[64,512]{1,0:T(8,128)(2,1)} %finish.1), channel_id=1, source_target_pairs={{0,10},{1,11},{2,8},{3,9},{4,14},{5,15},{6,12},{7,13},{8,2},{9,3},... | collective-permute-start | bytes 196616 | tf_op jit(solution)/shard_map/ppermute | solution.py:283
  212.6 7.9 %copy-start.14 = (bf16[64,512]{1,0:T(8,128)(2,1)}, bf16[64,512]{1,0:T(8,128)(2,1)S(1)}, u32[]{:S(2)}) copy-start(bf16[64,512]{1,0:T(8,128)(2,1)S(1)} %collective-permute-done.19.refs_7_) | copy-start | bytes 196612
  212.6 7.2 %collective-permute-start.17 = (bf16[64,512]{1,0:T(8,128)(2,1)}, bf16[64,512]{1,0:T(8,128)(2,1)S(1)}, u32[]{:S(2)}, u32[]{:S(2)}) collective-permute-start(bf16[64,512]{1,0:T(8,128)(2,1)} %finish.1), channel_id=1, source_target_pairs={{0,6},{1,7},{2,4},{3,5},{4,10},{5,11},{6,8},{7,9},{8,14},{9,15},{1... | collective-permute-start | bytes 196616 | tf_op jit(solution)/shard_map/ppermute | solution.py:283
  215.8 4.7 %copy-start.15 = (bf16[64,512]{1,0:T(8,128)(2,1)}, bf16[64,512]{1,0:T(8,128)(2,1)S(1)}, u32[]{:S(2)}) copy-start(bf16[64,512]{1,0:T(8,128)(2,1)S(1)} %collective-permute-done.18.refs_6_) | copy-start | bytes 196612
  215.8 4.6 %collective-permute-start.16 = (bf16[64,512]{1,0:T(8,128)(2,1)}, bf16[64,512]{1,0:T(8,128)(2,1)S(1)}, u32[]{:S(2)}, u32[]{:S(2)}) collective-permute-start(bf16[64,512]{1,0:T(8,128)(2,1)} %finish.1), channel_id=1, source_target_pairs={{0,2},{1,3},{2,0},{3,1},{4,6},{5,7},{6,4},{7,5},{8,10},{9,11},{10,... | collective-permute-start | bytes 196616 | tf_op jit(solution)/shard_map/ppermute | solution.py:283
  219.8 0.7 copy-start.16
  220.5 0.6 copy-start.17
  220.5 0.7 copy-start.10
  220.5 0.8 copy-start.11
  221.3 0.7 copy-start.12

commit v2 on v1

--- a/solution.py
+++ b/solution.py
@@ -7,7 +7,8 @@
 from jax.experimental.pallas import tpu as pltpu
 from jax.sharding import PartitionSpec as P
 
-TILE = 512
+TILE = 1024
+SMALL = 512
 RING = 4
 VMEM = 60 * 1024 * 1024
 ANY = pl.BlockSpec(memory_space=pl.ANY)
@@ -185,18 +186,18 @@
         out_ref[...] = sum_ref[...].astype(out_ref.dtype)
 
 
-def finish(hidden, gate, proj, offset, before, dtype, after):
-    span, rows = hidden.shape
+def finish(hidden, row, gate, proj, offset, before, dtype, after):
+    rows, span = gate.shape
     k = proj.shape[0]
-    first = offset // TILE
+    start, first = row // SMALL, offset // SMALL
     total = pl.BlockSpec((k, rows), lambda i: (0, 0))
     return pl.pallas_call(
         finish_kernel,
-        grid=(span // TILE,),
+        grid=(span // SMALL,),
         in_specs=[
-            pl.BlockSpec((TILE, rows), lambda i: (i, 0)),
-            pl.BlockSpec((rows, TILE), lambda i: (0, i)),
-            pl.BlockSpec((k, TILE), lambda i: (0, first + i)),
+            pl.BlockSpec((SMALL, rows), lambda i: (start + i, 0)),
+            pl.BlockSpec((rows, SMALL), lambda i: (0, i)),
+            pl.BlockSpec((k, SMALL), lambda i: (0, first + i)),
             total,
         ]
         + [ANY] * len(after),
@@ -247,8 +248,9 @@
 
 def chunks_of(hidden):
     units = hidden // TILE
-    last = 3 * TILE if hidden % TILE == 0 and units >= 8 else 0
-    return hidden - last, last
+    if hidden % TILE or units < 4:
+        return hidden, 0, 0
+    return hidden - 2 * TILE, TILE, TILE
 
 
 def on_device(n_dp, n_tensor, inputs, out_grad, gate_pre, down_weight, proj_in, proj_out, queries):
@@ -258,7 +260,7 @@
     shard = lax.axis_index("tensor").astype(jnp.int32).reshape(1)
     far, near = n_dp // 2, 1
     ring = n_tensor <= RING
-    main, extra = chunks_of(hidden)
+    main, last, start = chunks_of(hidden)
 
     def onward(piece, hold=None):
         if hold is not None:
@@ -286,13 +288,16 @@
     weights = (down_weight, swap(down_weight, "dp", n_dp, near))
     far_query = swap(queries, "dp", n_dp, far)
 
-    own_blocks = split_blocks(out_grad, 0, ())
+    start_gate = gate_pre[:, main + last :]
+    own_blocks = split_blocks(out_grad, 0, (start_gate,) if start else ())
     far_blocks = split_blocks(out_grad, n_dp // 2, (own_blocks,))
     far_blocks, _ = lax.optimization_barrier((far_blocks, far_query))
     far_start = swap(far_blocks, "dp", n_dp, far)
     own = [own_blocks, onward(own_blocks)] if ring and n_tensor > 1 else [own_blocks]
-    gates, far_start, own[-1] = lax.optimization_barrier(
-        ((gate_pre[:, :main], gate_pre[:, main:]), far_start, own[-1])
+    if start:
+        start_gate = swap(start_gate, "dp", n_dp, far)
+    gates, far_start, start_gate, _ = lax.optimization_barrier(
+        ((gate_pre[:, :main], gate_pre[:, main : main + last]), far_start, start_gate, own[-1])
     )
     far_gate, last_gate = (swap(part, "dp", n_dp, far) if part.size else None for part in gates)
 
@@ -312,7 +317,7 @@
             own.append(onward(own[-1]))
         own_early = list(enumerate(own))[:split]
         (own_sum,) = project(
-            shard, own_early, gate_pre, weights, proj_out, 0, hidden, 0, 0, None, None, ()
+            shard, own_early, gate_pre, weights, proj_out, 0, hidden, 0, 0, None, None, (own[-1],)
         )
         early_sum = own_sum
         pairs = all_pairs(early_sum)
@@ -326,11 +331,12 @@
         while len(own) < n_tensor:
             own.append(onward(own[-1], early_sum))
         own_late = list(enumerate(own))[split:]
-        middle = hidden // 2 if hidden % (2 * TILE) == 0 else hidden
+        middle = -(-hidden // (2 * TILE)) * TILE if hidden % TILE == 0 else hidden
         after = (partial,)
         for s in range(0, hidden, middle):
+            span = min(middle, hidden - s)
             (own_sum,) = project(
-                shard, own_late, gate_pre, weights, proj_out, s, middle, 0, s, own_sum, None, after
+                shard, own_late, gate_pre, weights, proj_out, s, span, 0, s, own_sum, None, after
             )
             if s == 0:
                 while len(others) < n_tensor:
@@ -349,16 +355,19 @@
         proj_in, inputs, (((0,), (1,)), ((), ())), preferred_element_type=jnp.float32
     )
     both = jnp.concatenate([input_part, own_sum])
-    places = [place for place, _ in far_late]
-    both, far_gate, pieces = lax.optimization_barrier((both, far_gate, [p for _, p in far_late]))
-    far_late = list(zip(places, pieces))
+    both, far_gate = lax.optimization_barrier((both, far_gate))
     terms = spread(both, 0)
 
     far_sum, *later = project(
-        shard, far_late, far_gate, weights, proj_out, 0, main, extra, 0, None, partial, (both,)
+        shard, far_late, far_gate, weights, proj_out, 0, main, last + start, 0, None, partial, (both,)
     )
-    if extra:
-        far_sum = finish(later[0], last_gate, proj_out, main, far_sum, jnp.bfloat16, ())
+    if later:
+        far_sum = finish(
+            later[0], last, start_gate, proj_out, main + last, far_sum, jnp.float32, ()
+        )
+        far_sum = finish(
+            later[0], 0, last_gate, proj_out, main, far_sum, jnp.bfloat16, tuple(terms[1:])
+        )
     return score(terms, spread(far_sum, far), pairs)
 
 

time: 227 us -> 236 us (1.040)
  waiting for transfers between devices: 51 us -> 65.4 us
  Pallas kernels: 133 us -> 128 us
    ppermute x7 -> x8, waiting for transfers between devices: 13.1 us -> 38.7 us  [swap(): return lax.ppermute(value, axis, [(i, i ^ mask) for i in range(size)])]
    ppermute x6, waiting for transfers between devices: 30.7 us -> 21.4 us  [onward(): lax.ppermute(piece, 'tensor', [(i, (i + 1) % n_tensor) for i in range(n_t...]
    pallas_call x5, Pallas kernels: 113 us -> 107 us  [project(): pl.pallas_call(functools.partial(project_kernel, tiles, ahead, len(pieces...]
    pallas_call x1 -> x2, Pallas kernels: 5.05 us -> 6.58 us  [finish(): pl.pallas_call(finish_kernel, grid=(span // SMALL,), in_specs=[pl.BlockSp...]
    ppermute x7 -> x8, starting transfers between devices: 5.77 us -> 6.62 us  [swap(): return lax.ppermute(value, axis, [(i, i ^ mask) for i in range(size)])]
  transfers between devices with their start and end apart: 20 -> 21, of which waited for: 10 -> 8; matrix products, arithmetic and copies ran while one was open for 7% -> 6% of each run, Pallas kernels for 57% -> 51%
where the time goes in v2:
time: 236 us
  Pallas kernels  128 us (54%)
  waiting for transfers between devices  65.4 us (28%)
  starting transfers between devices  22.7 us (10%)
  local copies, waits for them, and re-layouts  15.9 us (7%)
  other arithmetic  2.46 us (1%)
    pallas_call x5, Pallas kernels, project(): pl.pallas_call(functools.partial(project_kernel, tiles, ahead, len(pieces...  107 us
    ppermute x8, waiting for transfers between devices, swap(): return lax.ppermute(value, axis, [(i, i ^ mask) for i in range(size)])  38.7 us
    ppermute x6, waiting for transfers between devices, onward(): lax.ppermute(piece, 'tensor', [(i, (i + 1) % n_tensor) for i in range(n_t...  21.4 us
    pallas_call x2, Pallas kernels, split_blocks(): pl.pallas_call(functools.partial(split_kernel, first), grid=(4,), in_spec...  10.7 us
    ppermute x7, starting transfers between devices, spread(): got.append(lax.ppermute(value, ('tensor', 'dp'), pairs))  9.87 us
    ppermute x8, starting transfers between devices, swap(): return lax.ppermute(value, axis, [(i, i ^ mask) for i in range(size)])  6.62 us
    pallas_call x2, Pallas kernels, finish(): pl.pallas_call(finish_kernel, grid=(span // SMALL,), in_specs=[pl.BlockSp...  6.58 us
    ppermute x6, starting transfers between devices, onward(): lax.ppermute(piece, 'tensor', [(i, (i + 1) % n_tensor) for i in range(n_t...  6.25 us
  transfers between devices with their start and end apart: 21, of which 8 were waited for; matrix products, arithmetic and copies ran while one was open for 6% of the time, Pallas kernels for 51%

profile of v2, /device:TPU:0, one launch (start us, length us, event | category | flops | bytes accessed | tf_op | source)
XLA Modules:
  0.0 235.7 jit_solution(13707744588851608274)
XLA Ops:
  0.0 0.5 collective-permute-start.2
  0.5 3.1 %fusion = (bf16[512,1024]{1,0:T(8,128)(2,1)}, bf16[512,1024]{1,0:T(8,128)(2,1)}) fusion(bf16[512,7168]{1,0:T(8,128)(2,1)} %refs_6_.5), kind=kLoop, calls=%fused_computation.6 | loop fusion | bytes 4194304 | tf_op jit(solution)/shard_map/slice | solution.py:300
  3.5 5.4 %split_blocks.2.refs_0_ = bf16[2,512,512]{2,1,0:T(8,128)(2,1)} custom-call(bf16[512,4,512]{2,1,0:T(4,128)(2,1)} %grad_ref.3, bf16[512,1024]{1,0:T(8,128)(2,1)} %get-tuple-element.34.refs_0_), custom_call_target="tpu_custom_call" | custom-call | tf_op jit(solution)/shard_map/split_blocks/pallas_call | solution.py:37
  8.9 2.8 %collective-permute-start = (bf16[2,512,512]{2,1,0:T(8,128)(2,1)}, bf16[2,512,512]{2,1,0:T(8,128)(2,1)}, u32[]{:S(2)}, u32[]{:S(2)}) collective-permute-start(bf16[2,512,512]{2,1,0:T(8,128)(2,1)} %split_blocks.2.refs_0_), channel_id=1, source_target_pairs={{0,4},{4,8},{8,12},{12,0},{1,5},{5,9},{9,13},{13,1},{2,6},{6,10},{... | collective-permute-start | bytes 3145736 | tf_op jit(solution)/shard_map/ppermute | solution.py:268
  11.7 1.5 collective-permute-start.4
  13.1 0.5 collective-permute-start.6
  13.7 5.4 %split_blocks.3 = bf16[2,512,512]{2,1,0:T(8,128)(2,1)} custom-call(bf16[512,4,512]{2,1,0:T(4,128)(2,1)} %grad_ref.3, bf16[2,512,512]{2,1,0:T(8,128)(2,1)} %split_blocks.2.refs_0_), custom_call_target="tpu_custom_call" | custom-call | tf_op jit(solution)/shard_map/split_blocks/pallas_call | solution.py:37
  19.1 0.0 collective-permute-done.4
  19.1 1.5 collective-permute-start.5
  20.6 17.1 %collective-permute-done.refs_1_ = bf16[2,512,512]{2,1,0:T(8,128)(2,1)} collective-permute-done((bf16[2,512,512]{2,1,0:T(8,128)(2,1)}, bf16[2,512,512]{2,1,0:T(8,128)(2,1)}, u32[]{:S(2)}, u32[]{:S(2)}) %collective-permute-start) | collective-permute-done | bytes 1048608 | tf_op jit(solution)/shard_map/ppermute | solution.py:268
  37.6 0.0 collective-permute-start.1
  37.6 5.2 %slice.10 = bf16[512,5120]{1,0:T(8,128)(2,1)} slice(bf16[512,7168]{1,0:T(8,128)(2,1)} %refs_6_.5), slice={[0:512], [0:5120]} | slice | bytes 10485760 | tf_op jit(solution)/shard_map/slice | solution.py:300
  42.8 1.4 fusion.1
  44.2 0.0 collective-permute-done.6.gate_ref
  44.2 17.9 %collective-permute-done.5.refs_0_ = bf16[2,512,512]{2,1,0:T(8,128)(2,1)} collective-permute-done((bf16[2,512,512]{2,1,0:T(8,128)(2,1)}, bf16[2,512,512]{2,1,0:T(8,128)(2,1)}, u32[]{:S(2)}, u32[]{:S(2)}) %collective-permute-start.5) | collective-permute-done | bytes 1048608 | tf_op jit(solution)/shard_map/ppermute | solution.py:18
  62.1 1.6 collective-permute-start.7
  63.7 1.5 collective-permute-start.10
  65.2 0.0 collective-permute-done.1.refs_8_.refs_0_
  65.2 0.0 collective-permute-done.2.refs_3_.refs_5_
  65.2 1.0 copy-done.2
  66.2 26.3 %project.5.refs_6_.refs_8_ = f32[64,512]{1,0:T(8,128)} custom-call(s32[1]{0:T(128)} %bitcast.shard_ref, bf16[2,512,512]{2,1,0:T(8,128)(2,1)} %split_blocks.2.refs_0_, bf16[2,512,512]{2,1,0:T(8,128)(2,1)} %collective-permute-done.refs_1_, bf16[7168,2048]{1,0:T(8,128)(2,1)} %refs_4_.9, bf16[7168,2048]{1,0:T(8,128)(2,1)} %collective-permute-done.2.refs_3_.refs_5_, ...), custom_call_target="tpu_custom_call" | custom-call | flops 15032385536 | bytes 36700160 | tf_op jit(solution)/shard_map/project/pallas_call | solution.py:151
  92.5 0.1 collective-permute-start.8
  92.6 0.5 collective-permute-start.9
  93.1 1.6 collective-permute-start.3
  94.6 0.3 collective-permute-start.14
  95.0 22.8 %project.6.refs_9_.refs_8_ = f32[7168,512]{1,0:T(8,128)} custom-call(s32[1]{0:T(128)} %bitcast.shard_ref, bf16[2,512,512]{2,1,0:T(8,128)(2,1)} %collective-permute-done.5.refs_0_, bf16[2,512,512]{2,1,0:T(8,128)(2,1)} %collective-permute-done.7.refs_1_, bf16[7168,2048]{1,0:T(8,128)(2,1)} %refs_4_.9, ...), custom_call_target="tpu_custom_call" | custom-call | flops 15032385536 | bytes 36700160 | tf_op jit(solution)/shard_map/project/pallas_call | solution.py:151
  117.9 0.6 collective-permute-start.16
  118.5 0.0 collective-permute-done.9
  118.6 1.1 reshape.10
  119.7 0.7 copy.8
  120.4 0.7 collective-permute-done.3.refs_1_
  121.1 1.0 copy-done.3
  122.1 17.2 %project.7.refs_8_ = f32[64,512]{1,0:T(8,128)} custom-call(s32[1]{0:T(128)} %bitcast.shard_ref, bf16[2,512,512]{2,1,0:T(8,128)(2,1)} %copy-done.2, bf16[2,512,512]{2,1,0:T(8,128)(2,1)} %copy-done.3, bf16[7168,2048]{1,0:T(8,128)(2,1)} %refs_4_.9, bf16[7168,2048]{1,0:T(8,128)(2,1)} %collective-permute-done.2.refs_3_.refs_5_, bf16[7168,2048]{1,0:T(8,128)(2,1)} %refs_4_.9, ...), custom_call_target="tpu_custom_call" | custom-call | flops 8589934592 | bytes 20971520 | tf_op jit(solution)/shard_map/project/pallas_call | solution.py:151
  139.3 3.5 %collective-permute-done.14.refs_0_ = bf16[2,512,512]{2,1,0:T(8,128)(2,1)} collective-permute-done((bf16[2,512,512]{2,1,0:T(8,128)(2,1)}, bf16[2,512,512]{2,1,0:T(8,128)(2,1)}, u32[]{:S(2)}, u32[]{:S(2)}) %collective-permute-start.14) | collective-permute-done | bytes 1048608 | tf_op jit(solution)/shard_map/ppermute | solution.py:268
  142.8 0.0 collective-permute-start.15
  142.8 1.5 pad_maximum_fusion.refs_9_.refs_8_
  144.3 14.0 %project.8 = f32[64,512]{1,0:T(8,128)} custom-call(s32[1]{0:T(128)} %bitcast.shard_ref, bf16[2,512,512]{2,1,0:T(8,128)(2,1)} %copy-done.2, bf16[2,512,512]{2,1,0:T(8,128)(2,1)} %copy-done.3, bf16[7168,2048]{1,0:T(8,128)(2,1)} %refs_4_.9, bf16[7168,2048]{1,0:T(8,128)(2,1)} %collective-permute-done.2.refs_3_.refs_5_, bf16[7168,2048]{1,0:T(8,128)(2,1)} %refs_4_.9, ...), custom_call_target="tpu_custom_call" | custom-call | flops 6442450944 | bytes 15728640 | tf_op jit(solution)/shard_map/project/pallas_call | solution.py:151
  158.3 0.9 pad_maximum_fusion.1.refs_9_.refs_0_
  159.3 20.8 %collective-permute-done.10.refs_6_ = bf16[512,5120]{1,0:T(8,128)(2,1)} collective-permute-done((bf16[512,5120]{1,0:T(8,128)(2,1)}, bf16[512,5120]{1,0:T(8,128)(2,1)}, u32[]{:S(2)}, u32[]{:S(2)}) %collective-permute-start.10) | collective-permute-done | bytes 5242912 | tf_op jit(solution)/shard_map/ppermute | solution.py:18
  180.0 2.2 collective-permute-start.13
  182.3 0.8 collective-permute-start.12
  183.1 0.3 collective-permute-start.11
  183.3 0.0 collective-permute-done.15.refs_1_
  183.4 1.0 copy-done.5
  184.3 26.4 %project.9 = (f32[64,512]{1,0:T(8,128)}, f32[2048,512]{1,0:T(8,128)}) custom-call(s32[1]{0:T(128)} %bitcast.shard_ref, bf16[2,512,512]{2,1,0:T(8,128)(2,1)} %collective-permute-done.14.refs_0_, bf16[2,512,512]{2,1,0:T(8,128)(2,1)} %copy-done.5, bf16[7168,2048]{1,0:T(8,128)(2,1)} %refs_4_.9, bf16[7168,2048]{1,0:T(8,128)(2,1)} %collective-permute-done.2.refs_3_.refs_5_, ...), custom_call_target="tpu_custom_call" | custom-call | flops 15032385536 | bytes 36700160 | tf_op jit(solution)/shard_map/project/pallas_call | solution.py:151
  210.8 3.4 %finish.2.before_ref = f32[64,512]{1,0:T(8,128)} custom-call(f32[2048,512]{1,0:T(8,128)} %get-tuple-element.29.hidden_ref, bf16[512,1024]{1,0:T(8,128)(2,1)} %collective-permute-done.6.gate_ref, bf16[64,7168]{1,0:T(8,128)(2,1)} %bitcast.10, f32[64,512]{1,0:T(8,128)} %get-tuple-element.32.before_ref), custom_call_target="tpu_custom_call" | custom-call | tf_op jit(solution)/shard_map/finish/pallas_call | solution.py:194
  214.1 0.0 collective-permute-done.16.gate_ref
  214.2 0.0 collective-permute-done.13.refs_2_.refs_3_
  214.2 0.0 collective-permute-done.12.refs_1_.refs_2_
  214.2 0.7 copy-done.6
  214.9 0.1 copy-done.7
  215.0 0.7 copy-done.8
  215.7 3.2 %finish.3 = bf16[64,512]{1,0:T(8,128)(2,1)} custom-call(f32[2048,512]{1,0:T(8,128)} %get-tuple-element.29.hidden_ref, bf16[512,1024]{1,0:T(8,128)(2,1)} %collective-permute-done.16.gate_ref, bf16[64,7168]{1,0:T(8,128)(2,1)} %bitcast.11, f32[64,512]{1,0:T(8,128)} %finish.2.before_ref, f32[128,512]{1,0:T(8,128)} %copy-done.8, f32[128,512]{1,0:T(8,128)} %copy-done.7, ...), custom_call_target="tpu_custom_call" | custom-call | tf_op jit(solution)/shard_map/finish/pallas_call | solution.py:194
  218.9 4.5 %collective-permute-start.20 = (bf16[64,512]{1,0:T(8,128)(2,1)}, bf16[64,512]{1,0:T(8,128)(2,1)S(1)}, u32[]{:S(2)}, u32[]{:S(2)}) collective-permute-start(bf16[64,512]{1,0:T(8,128)(2,1)} %finish.3), channel_id=1, source_target_pairs={{0,14},{1,15},{2,12},{3,13},{4,2},{5,3},{6,0},{7,1},{8,6},{9,7},{1... | collective-permute-start | bytes 196616 | tf_op jit(solution)/shard_map/ppermute | solution.py:285
  223.4 0.2 collective-permute-start.19
  223.6 0.9 collective-permute-start.18
  224.6 0.9 collective-permute-start.17
  225.4 0.2 collective-permute-done.20.refs_7_
  225.6 4.1 %collective-permute-done.19.refs_6_ = bf16[64,512]{1,0:T(8,128)(2,1)S(1)} collective-permute-done((bf16[64,512]{1,0:T(8,128)(2,1)}, bf16[64,512]{1,0:T(8,128)(2,1)S(1)}, u32[]{:S(2)}, u32[]{:S(2)}) %collective-permute-start.19) | collective-permute-done | bytes 65568 | tf_op jit(solution)/shard_map/ppermute | solution.py:285
  229.8 1.1 collective-permute-done.18.refs_5_
  230.8 0.0 collective-permute-done.17.refs_4_
  230.8 0.6 copy-done.16
  231.5 0.6 copy-done.17
  232.1 3.6 %score.1 = f32[64,512]{1,0:T(8,128)} custom-call(f32[128,512]{1,0:T(8,128)} %copy-done.4, f32[128,512]{1,0:T(8,128)} %copy-done.8, f32[128,512]{1,0:T(8,128)} %copy-done.7, f32[128,512]{1,0:T(8,128)} %copy-done.6, bf16[64,512]{1,0:T(8,128)(2,1)} %copy-done.17, bf16[64,512]{1,0:T(8,128)(2,1)} %copy-done.16, bf16[64,512]{1,0:T(8,128)(2,1)} %copy-done.15, ...), custom_call_target="tpu_custom_call" | custom-call | tf_op jit(solution)/shard_map/score/pallas_call | solution.py:241
  (36 shorter events, 0.2 us)
Async XLA Ops:
  0.0 42.8 %copy-start = (bf16[512,2048]{1,0:T(8,128)(2,1)S(1)}, bf16[512,2048]{1,0:T(8,128)(2,1)}, u32[]{:S(2)}) copy-start(bf16[512,2048]{1,0:T(8,128)(2,1)} %param.7) | copy-start | bytes 6291460
  0.0 11.6 %copy-start.11 = (bf16[64,1024]{1,0:T(8,128)(2,1)S(1)}, bf16[64,1024]{1,0:T(8,128)(2,1)}, u32[]{:S(2)}) copy-start(bf16[64,1024]{1,0:T(8,128)(2,1)} %param.13) | copy-start | bytes 393220
  0.0 65.2 %collective-permute-start.2 = (bf16[7168,2048]{1,0:T(8,128)(2,1)}, bf16[7168,2048]{1,0:T(8,128)(2,1)}, u32[]{:S(2)}, u32[]{:S(2)}) collective-permute-start(bf16[7168,2048]{1,0:T(8,128)(2,1)} %refs_4_.9), channel_id=1, source_target_pairs={{0,1},{1,0},{2,3},{3,2},{4,5},{5,4},{6,7},{7,6},{8,9},{9,8},{10,11... | collective-permute-start | bytes 88080392 | tf_op jit(solution)/shard_map/ppermute | solution.py:18
  8.9 28.8 %collective-permute-start = (bf16[2,512,512]{2,1,0:T(8,128)(2,1)}, bf16[2,512,512]{2,1,0:T(8,128)(2,1)}, u32[]{:S(2)}, u32[]{:S(2)}) collective-permute-start(bf16[2,512,512]{2,1,0:T(8,128)(2,1)} %split_blocks.2.refs_0_), channel_id=1, source_target_pairs={{0,4},{4,8},{8,12},{12,0},{1,5},{5,9},{9,13},{13,1},{2,6},{6,10},{... | collective-permute-start | bytes 3145736 | tf_op jit(solution)/shard_map/ppermute | solution.py:268
  11.7 7.4 %collective-permute-start.4 = (bf16[64,1024]{1,0:T(8,128)(2,1)S(1)}, bf16[64,1024]{1,0:T(8,128)(2,1)S(1)}, u32[]{:S(2)}, u32[]{:S(2)}) collective-permute-start(bf16[64,1024]{1,0:T(8,128)(2,1)S(1)} %copy-done.11), channel_id=1, source_target_pairs={{0,2},{1,3},{2,0},{3,1},{4,6},{5,7},{6,4},{7,5},{8,10},{9,11},{10,... | collective-permute-start | bytes 393224 | tf_op jit(solution)/shard_map/ppermute | solution.py:18
  13.1 31.1 %collective-permute-start.6 = (bf16[512,1024]{1,0:T(8,128)(2,1)}, bf16[512,1024]{1,0:T(8,128)(2,1)}, u32[]{:S(2)}, u32[]{:S(2)}) collective-permute-start(bf16[512,1024]{1,0:T(8,128)(2,1)} %get-tuple-element.34.refs_0_), channel_id=1, source_target_pairs={{0,2},{1,3},{2,0},{3,1},{4,6},{5,7},{6,4},{7,5},{8,10},{9,11},{10,... | collective-permute-start | bytes 3145736 | tf_op jit(solution)/shard_map/ppermute | solution.py:18
  19.1 1.5 copy-start.12
  19.1 43.1 %collective-permute-start.5 = (bf16[2,512,512]{2,1,0:T(8,128)(2,1)}, bf16[2,512,512]{2,1,0:T(8,128)(2,1)}, u32[]{:S(2)}, u32[]{:S(2)}) collective-permute-start(bf16[2,512,512]{2,1,0:T(8,128)(2,1)} %split_blocks.3), channel_id=1, source_target_pairs={{0,2},{1,3},{2,0},{3,1},{4,6},{5,7},{6,4},{7,5},{8,10},{9,11},{10,... | collective-permute-start | bytes 3145736 | tf_op jit(solution)/shard_map/ppermute | solution.py:18
  37.6 27.6 %collective-permute-start.1 = (bf16[2,512,512]{2,1,0:T(8,128)(2,1)}, bf16[2,512,512]{2,1,0:T(8,128)(2,1)S(1)}, u32[]{:S(2)}, u32[]{:S(2)}) collective-permute-start(bf16[2,512,512]{2,1,0:T(8,128)(2,1)} %collective-permute-done.refs_1_), channel_id=1, source_target_pairs={{0,4},{4,8},{8,12},{12,0},{1,5},{5,9},{9,13},{13,1},{2,6},{6,10},{... | collective-permute-start | bytes 3145736 | tf_op jit(solution)/shard_map/ppermute | solution.py:268
  37.6 5.2 %copy-start.10 = (bf16[2048,64]{0,1:T(8,128)(2,1)S(1)}, bf16[2048,64]{0,1:T(8,128)(2,1)}, u32[]{:S(2)}) copy-start(bf16[2048,64]{0,1:T(8,128)(2,1)} %param.11) | copy-start | bytes 786436
  62.1 30.3 %collective-permute-start.7 = (bf16[2,512,512]{2,1,0:T(8,128)(2,1)}, bf16[2,512,512]{2,1,0:T(8,128)(2,1)}, u32[]{:S(2)}, u32[]{:S(2)}) collective-permute-start(bf16[2,512,512]{2,1,0:T(8,128)(2,1)} %collective-permute-done.5.refs_0_), channel_id=1, source_target_pairs={{0,4},{4,8},{8,12},{12,0},{1,5},{5,9},{9,13},{13,1},{2,6},{6,10},{... | collective-permute-start | bytes 3145736 | tf_op jit(solution)/shard_map/ppermute | solution.py:268
  63.7 116.3 %collective-permute-start.10 = (bf16[512,5120]{1,0:T(8,128)(2,1)}, bf16[512,5120]{1,0:T(8,128)(2,1)}, u32[]{:S(2)}, u32[]{:S(2)}) collective-permute-start(bf16[512,5120]{1,0:T(8,128)(2,1)} %slice.10), channel_id=1, source_target_pairs={{0,2},{1,3},{2,0},{3,1},{4,6},{5,7},{6,4},{7,5},{8,10},{9,11},{10,... | collective-permute-start | bytes 15728648 | tf_op jit(solution)/shard_map/ppermute | solution.py:18
  65.2 1.0 copy-start.2
  66.2 26.4 %copy-start.13 = (bf16[64,1024]{1,0:T(8,128)(2,1)S(1)}, bf16[64,1024]{1,0:T(8,128)(2,1)}, u32[]{:S(2)}) copy-start(bf16[64,1024]{1,0:T(8,128)(2,1)} %copy-done.12) | copy-start | bytes 393220
  92.5 25.4 %collective-permute-start.8 = (bf16[64,1024]{1,0:T(8,128)(2,1)S(1)}, bf16[64,1024]{1,0:T(8,128)(2,1)S(1)}, u32[]{:S(2)}, u32[]{:S(2)}) collective-permute-start(bf16[64,1024]{1,0:T(8,128)(2,1)S(1)} %copy-done.11), channel_id=1, source_target_pairs={{0,1},{1,0},{2,3},{3,2},{4,5},{5,4},{6,7},{7,6},{8,9},{9,8},{10,11... | collective-permute-start | bytes 393224 | tf_op jit(solution)/shard_map/ppermute | solution.py:18
  92.6 25.9 %collective-permute-start.9 = (bf16[64,1024]{1,0:T(8,128)(2,1)S(1)}, bf16[64,1024]{1,0:T(8,128)(2,1)S(1)}, u32[]{:S(2)}, u32[]{:S(2)}) collective-permute-start(bf16[64,1024]{1,0:T(8,128)(2,1)S(1)} %copy-done.13), channel_id=1, source_target_pairs={{0,1},{1,0},{2,3},{3,2},{4,5},{5,4},{6,7},{7,6},{8,9},{9,8},{10,11... | collective-permute-start | bytes 393224 | tf_op jit(solution)/shard_map/ppermute | solution.py:18
  93.1 28.0 %collective-permute-start.3 = (bf16[2,512,512]{2,1,0:T(8,128)(2,1)}, bf16[2,512,512]{2,1,0:T(8,128)(2,1)S(1)}, u32[]{:S(2)}, u32[]{:S(2)}) collective-permute-start(bf16[2,512,512]{2,1,0:T(8,128)(2,1)} %copy-done.2), channel_id=1, source_target_pairs={{0,4},{4,8},{8,12},{12,0},{1,5},{5,9},{9,13},{13,1},{2,6},{6,10},{... | collective-permute-start | bytes 3145736 | tf_op jit(solution)/shard_map/ppermute | solution.py:268
  94.6 48.2 %collective-permute-start.14 = (bf16[2,512,512]{2,1,0:T(8,128)(2,1)}, bf16[2,512,512]{2,1,0:T(8,128)(2,1)}, u32[]{:S(2)}, u32[]{:S(2)}) collective-permute-start(bf16[2,512,512]{2,1,0:T(8,128)(2,1)} %collective-permute-done.7.refs_1_), channel_id=1, source_target_pairs={{0,4},{4,8},{8,12},{12,0},{1,5},{5,9},{9,13},{13,1},{2,6},{6,10},{... | collective-permute-start | bytes 3145736 | tf_op jit(solution)/shard_map/ppermute | solution.py:268
  117.9 96.2 %collective-permute-start.16 = (bf16[512,1024]{1,0:T(8,128)(2,1)}, bf16[512,1024]{1,0:T(8,128)(2,1)}, u32[]{:S(2)}, u32[]{:S(2)}) collective-permute-start(bf16[512,1024]{1,0:T(8,128)(2,1)} %get-tuple-element.30), channel_id=1, source_target_pairs={{0,2},{1,3},{2,0},{3,1},{4,6},{5,7},{6,4},{7,5},{8,10},{9,11},{10,... | collective-permute-start | bytes 3145736 | tf_op jit(solution)/shard_map/ppermute | solution.py:18
  121.1 1.0 copy-start.3
  142.8 40.5 %collective-permute-start.15 = (bf16[2,512,512]{2,1,0:T(8,128)(2,1)}, bf16[2,512,512]{2,1,0:T(8,128)(2,1)S(1)}, u32[]{:S(2)}, u32[]{:S(2)}) collective-permute-start(bf16[2,512,512]{2,1,0:T(8,128)(2,1)} %collective-permute-done.14.refs_0_), channel_id=1, source_target_pairs={{0,4},{4,8},{8,12},{12,0},{1,5},{5,9},{9,13},{13,1},{2,6},{6,10},{... | collective-permute-start | bytes 3145736 | tf_op jit(solution)/shard_map/ppermute | solution.py:268
  144.3 14.0 %copy-start.9 = (f32[64,512]{1,0:T(8,128)S(1)}, f32[64,512]{1,0:T(8,128)}, u32[]{:S(2)}) copy-start(f32[64,512]{1,0:T(8,128)} %fusion.1) | copy-start | bytes 393220
  159.2 24.1 %copy-start.4 = (f32[128,512]{1,0:T(8,128)}, f32[128,512]{1,0:T(8,128)S(1)}, u32[]{:S(2)}) copy-start(f32[128,512]{1,0:T(8,128)S(1)} %pad_maximum_fusion.1.refs_9_.refs_0_) | copy-start | bytes 786436
  180.0 34.1 %collective-permute-start.13 = (f32[128,512]{1,0:T(8,128)S(1)}, f32[128,512]{1,0:T(8,128)S(1)}, u32[]{:S(2)}, u32[]{:S(2)}) collective-permute-start(f32[128,512]{1,0:T(8,128)S(1)} %pad_maximum_fusion.1.refs_9_.refs_0_), channel_id=1, source_target_pairs={{0,12},{1,13},{2,14},{3,15},{4,0},{5,1},{6,2},{7,3},{8,4},{9,5},{1... | collective-permute-start | bytes 786440 | tf_op jit(solution)/shard_map/ppermute | solution.py:285
  182.3 31.9 %collective-permute-start.12 = (f32[128,512]{1,0:T(8,128)S(1)}, f32[128,512]{1,0:T(8,128)S(1)}, u32[]{:S(2)}, u32[]{:S(2)}) collective-permute-start(f32[128,512]{1,0:T(8,128)S(1)} %pad_maximum_fusion.1.refs_9_.refs_0_), channel_id=1, source_target_pairs={{0,8},{1,9},{2,10},{3,11},{4,12},{5,13},{6,14},{7,15},{8,0},{9,1},... | collective-permute-start | bytes 786440 | tf_op jit(solution)/shard_map/ppermute | solution.py:285
  183.1 31.1 %collective-permute-start.11 = (f32[128,512]{1,0:T(8,128)S(1)}, f32[128,512]{1,0:T(8,128)S(1)}, u32[]{:S(2)}, u32[]{:S(2)}) collective-permute-start(f32[128,512]{1,0:T(8,128)S(1)} %pad_maximum_fusion.1.refs_9_.refs_0_), channel_id=1, source_target_pairs={{0,4},{1,5},{2,6},{3,7},{4,8},{5,9},{6,10},{7,11},{8,12},{9,13},{1... | collective-permute-start | bytes 786440 | tf_op jit(solution)/shard_map/ppermute | solution.py:285
  183.3 1.0 copy-start.5
  210.8 24.9 %copy-start.1 = (bf16[512,2048]{1,0:T(8,128)(2,1)S(1)}, bf16[512,2048]{1,0:T(8,128)(2,1)}, u32[]{:S(2)}) copy-start(bf16[512,2048]{1,0:T(8,128)(2,1)} %param.7) | copy-start | bytes 6291460
  214.2 0.7 copy-start.6
  214.2 0.8 copy-start.7
  215.0 0.7 copy-start.8
  218.9 6.7 %collective-permute-start.20 = (bf16[64,512]{1,0:T(8,128)(2,1)}, bf16[64,512]{1,0:T(8,128)(2,1)S(1)}, u32[]{:S(2)}, u32[]{:S(2)}) collective-permute-start(bf16[64,512]{1,0:T(8,128)(2,1)} %finish.3), channel_id=1, source_target_pairs={{0,14},{1,15},{2,12},{3,13},{4,2},{5,3},{6,0},{7,1},{8,6},{9,7},{1... | collective-permute-start | bytes 196616 | tf_op jit(solution)/shard_map/ppermute | solution.py:285
  223.4 6.3 %collective-permute-start.19 = (bf16[64,512]{1,0:T(8,128)(2,1)}, bf16[64,512]{1,0:T(8,128)(2,1)S(1)}, u32[]{:S(2)}, u32[]{:S(2)}) collective-permute-start(bf16[64,512]{1,0:T(8,128)(2,1)} %finish.3), channel_id=1, source_target_pairs={{0,10},{1,11},{2,8},{3,9},{4,14},{5,15},{6,12},{7,13},{8,2},{9,3},... | collective-permute-start | bytes 196616 | tf_op jit(solution)/shard_map/ppermute | solution.py:285
  223.6 7.2 %collective-permute-start.18 = (bf16[64,512]{1,0:T(8,128)(2,1)}, bf16[64,512]{1,0:T(8,128)(2,1)S(1)}, u32[]{:S(2)}, u32[]{:S(2)}) collective-permute-start(bf16[64,512]{1,0:T(8,128)(2,1)} %finish.3), channel_id=1, source_target_pairs={{0,6},{1,7},{2,4},{3,5},{4,10},{5,11},{6,8},{7,9},{8,14},{9,15},{1... | collective-permute-start | bytes 196616 | tf_op jit(solution)/shard_map/ppermute | solution.py:285
  224.6 6.2 %collective-permute-start.17 = (bf16[64,512]{1,0:T(8,128)(2,1)}, bf16[64,512]{1,0:T(8,128)(2,1)S(1)}, u32[]{:S(2)}, u32[]{:S(2)}) collective-permute-start(bf16[64,512]{1,0:T(8,128)(2,1)} %finish.3), channel_id=1, source_target_pairs={{0,2},{1,3},{2,0},{3,1},{4,6},{5,7},{6,4},{7,5},{8,10},{9,11},{10,... | collective-permute-start | bytes 196616 | tf_op jit(solution)/shard_map/ppermute | solution.py:285
  225.6 5.2 %copy-start.14 = (bf16[64,512]{1,0:T(8,128)(2,1)}, bf16[64,512]{1,0:T(8,128)(2,1)S(1)}, u32[]{:S(2)}) copy-start(bf16[64,512]{1,0:T(8,128)(2,1)S(1)} %collective-permute-done.20.refs_7_) | copy-start | bytes 196612
  229.8 1.1 copy-start.15
  230.8 0.6 copy-start.16
  231.5 0.6 copy-start.17
